TPU v7x, 32 devices: a whole 2x2x4 slice. The times are simulated.
32 devices in a mesh: groups: 2 (over y), ctx: 4 (over z), dom: 2 (over x), tp: 2 (over core).
Axes of the slice: x: 2, y: 2, z: 4, core: 2. Of those that a mesh axis runs over, the one named last changes fastest.
Arguments:
- queries: bfloat16 [8, 32, 8, 8, 128], P('groups', 'dom', 'tp'), parts along dimension 0, may hold values from -8 to 8
- prompt_cache: bfloat16 [4, 8192, 8, 128], P('groups', 'ctx', 'tp'), parts along dimension 0, may hold values from -8 to 8
- suffix_cache: bfloat16 [4, 32, 16, 8, 128], P('groups', 'dom', 'ctx', 'tp'), parts along dimension 0, may hold values from -8 to 8
- new_kv: bfloat16 [8, 2, 32, 8, 128], P('groups', None, 'dom', 'tp'), parts along dimension 0, may hold values from -8 to 8
- ancestors: int32 [8, 32], P('groups'), parts along dimension 0, may hold values from 0 to 31, as said below
- lengths: int32 [64], P('groups'), parts along dimension 0, may hold values from 1 to 12, as said below
Outputs:
- attended: bfloat16 [8, 32, 8, 8, 128], P('groups', 'dom', 'tp'), parts along dimension 0
There are 2 independent parts, one for each index of `groups`. A program takes and returns all parts, laid end to end along the dimension named above; each array names one. Nothing has to cross between parts.
Inputs may be any that keep to these rules, and one draw needn't show every extreme that they name: `ancestors`: particle p is owned by owner p // 16. In every step, of the 16 offspring of one owner at most 16 have their ancestor among the particles of any one owner, and each owner has exactly 16 from some one owner. `lengths`: the largest length is reached in every draw.
All inputs are finite; a program needn't handle non-finite values.
Results may differ from a plain program's by a relative error of at most 0.005.
Values may be sent and summed in bfloat16 or wider, within the bound.
No kernel may reach another device: no remote copies, remote signals or barrier semaphores. Data moves between devices by JAX's collectives and lax.ppermute only.
A program may use at most 128 MiB of HBM per device.

v0:
```python
import math

import jax
import jax.numpy as jnp
from jax import lax
from jax.sharding import PartitionSpec as P


def resample_whole(flat_rows, my_parents, particles):
    one_hot = (my_parents[:, None] == jnp.arange(particles, dtype=jnp.int32)[None, :]).astype(
        jnp.bfloat16
    )
    gathered = jnp.einsum(
        "ji,cir->cjr",
        one_hot,
        lax.all_gather(flat_rows, "dom", axis=1, tiled=True),
        preferred_element_type=jnp.float32,
    )
    return gathered.astype(jnp.bfloat16)


def attend(query_block, prompt_keys, prompt_values, suffix_rows, visible, score_scale):
    prompt_scores = (
        jnp.einsum("pkgh,tkh->kpgt", query_block, prompt_keys, preferred_element_type=jnp.float32)
        * score_scale
    )
    suffix_scores = (
        jnp.einsum(
            "pkgh,pskh->pkgs", query_block, suffix_rows[0], preferred_element_type=jnp.float32
        )
        * score_scale
    )
    suffix_scores = jnp.where(visible[:, None, None, :], suffix_scores, -jnp.inf)
    local_peak = jnp.maximum(
        jnp.transpose(jnp.max(prompt_scores, axis=-1), (1, 0, 2)), jnp.max(suffix_scores, axis=-1)
    )
    peak_score = lax.pmax(local_peak, "ctx")
    prompt_exp = jnp.exp(prompt_scores - jnp.transpose(peak_score, (1, 0, 2))[..., None])
    suffix_exp = jnp.exp(suffix_scores - peak_score[..., None])
    totals = jnp.transpose(jnp.sum(prompt_exp, axis=-1), (1, 0, 2)) + jnp.sum(suffix_exp, axis=-1)
    prompt_weights = prompt_exp.astype(jnp.bfloat16)
    suffix_weights = suffix_exp.astype(jnp.bfloat16)
    numerator = jnp.einsum(
        "kpgt,tkh->pkgh", prompt_weights, prompt_values, preferred_element_type=jnp.float32
    )
    numerator = numerator + jnp.einsum(
        "pkgs,pskh->pkgh", suffix_weights, suffix_rows[1], preferred_element_type=jnp.float32
    )
    total_all, numerator_all = lax.psum((totals, numerator), "ctx")
    return (numerator_all / total_all[..., None]).astype(jnp.bfloat16)


def on_device(queries, prompt_cache, suffix_cache, new_kv, ancestors, lengths):
    my_owner = lax.axis_index("dom")
    my_shard = lax.axis_index("ctx")
    per_owner = queries.shape[1]
    suffix_dev = suffix_cache.shape[2]
    particles = ancestors.shape[1]
    score_scale = 1.0 / math.sqrt(queries.shape[4])
    prompt_keys = prompt_cache[0]
    prompt_values = prompt_cache[1]
    particle_ids = jnp.arange(particles, dtype=jnp.int32)
    positions = my_shard * suffix_dev + jnp.arange(suffix_dev, dtype=jnp.int32)
    suffix_rows = suffix_cache
    lengths_now = lengths
    results = []
    for step_index in range(queries.shape[0]):
        parents = ancestors[step_index]
        my_parents = lax.dynamic_slice_in_dim(parents, my_owner * per_owner, per_owner)
        flat_rows = suffix_rows.reshape(2, per_owner, -1)
        moved_rows = resample_whole(flat_rows, my_parents, particles)
        suffix_rows = moved_rows.reshape(suffix_rows.shape)
        lengths_now = jnp.sum(
            jnp.where(parents[:, None] == particle_ids[None, :], lengths_now[None, :], 0), axis=1
        )
        my_lengths = lax.dynamic_slice_in_dim(lengths_now, my_owner * per_owner, per_owner)
        new_slot = positions[None, :] == my_lengths[:, None]
        suffix_rows = jnp.where(
            new_slot[None, :, :, None, None], new_kv[step_index][:, :, None], suffix_rows
        )
        visible = positions[None, :] <= my_lengths[:, None]
        results.append(
            attend(
                queries[step_index], prompt_keys, prompt_values, suffix_rows, visible, score_scale
            )
        )
        lengths_now = lengths_now + 1
    return jnp.stack(results)


def solution(mesh):
    return jax.shard_map(
        on_device,
        mesh=mesh,
        in_specs=(
            P("groups", "dom", "tp", None, None),
            P("groups", "ctx", "tp", None),
            P("groups", "dom", "ctx", "tp", None),
            P("groups", None, "dom", "tp", None),
            P("groups", None),
            P("groups"),
        ),
        out_specs=P("groups", "dom", "tp", None, None),
        check_vma=False,
    )
```

profile of v0, /device:TPU:0, one launch (start us, length us, event | category | flops | bytes accessed | tf_op | source)
XLA Modules:
  0.0 164.5 jit_solution(15562038349087660170)
XLA Ops:
  6.5 0.8 slice_bitcast_fusion.16
  7.4 0.8 select_reduce_fusion.3
  8.8 4.1 %fusion.100 = (bf16[1,2048,4,128]{3,2,1,0:T(4,128)(2,1)S(1)}, bf16[1,2048,4,128]{3,2,1,0:T(4,128)(2,1)}) fusion(bf16[2,2048,4,128]{3,2,1,0:T(4,128)(2,1)} %param.7), kind=kLoop, calls=%fused_computation.178 | loop fusion | bytes 8388608 | tf_op jit(solution)/shard_map/slice | solution.py:60
  12.9 0.8 fusion.101
  13.7 0.6 slice_bitcast_fusion.12
  14.4 0.6 copy-done.15
  15.4 0.7 broadcast_compare_fusion.7
  17.0 7.1 %all_gather.12 = bf16[2,32,2048]{2,1,0:T(8,128)(2,1)S(1)} all-gather(bf16[2,16,2048]{2,1,0:T(8,128)(2,1)S(1)} %reshape.274), channel_id=1, replica_groups=mesh['groups'=2,'ctx'=4,'dom'=2,'tp'=2] {'dom'}, dimensions={1}, use_global_device_ids=true | all-gather | bytes 393216 | tf_op jit(solution)/shard_map/all_gather | solution.py:16
  24.4 5.6 %all_gather.13 = bf16[2,32,2048]{2,1,0:T(8,128)(2,1)S(1)} all-gather(bf16[2,16,2048]{2,1,0:T(8,128)(2,1)S(1)} %get-tuple-element.59), channel_id=1, replica_groups=mesh['groups'=2,'ctx'=4,'dom'=2,'tp'=2] {'dom'}, dimensions={1}, use_global_device_ids=true | all-gather | bytes 393216 | tf_op jit(solution)/shard_map/all_gather | solution.py:16
  30.1 0.2 broadcast_select_fusion.1
  30.3 5.6 %all_gather.14 = bf16[2,32,2048]{2,1,0:T(8,128)(2,1)S(1)} all-gather(bf16[2,16,2048]{2,1,0:T(8,128)(2,1)S(1)} %get-tuple-element.61), channel_id=1, replica_groups=mesh['groups'=2,'ctx'=4,'dom'=2,'tp'=2] {'dom'}, dimensions={1}, use_global_device_ids=true | all-gather | bytes 393216 | tf_op jit(solution)/shard_map/all_gather | solution.py:16
  36.3 5.8 %all_gather.15 = bf16[2,32,2048]{2,1,0:T(8,128)(2,1)S(1)} all-gather(bf16[2,16,2048]{2,1,0:T(8,128)(2,1)S(1)} %get-tuple-element.63), channel_id=1, replica_groups=mesh['groups'=2,'ctx'=4,'dom'=2,'tp'=2] {'dom'}, dimensions={1}, use_global_device_ids=true | all-gather | bytes 393216 | tf_op jit(solution)/shard_map/all_gather | solution.py:16
  42.5 4.1 %multiply_reduce_fusion = (f32[4,16,8]{2,1,0:T(8,128)}, f32[4,16,8,2048]{3,2,1,0:T(8,128)}) fusion(bf16[1,2048,4,128]{3,2,1,0:T(4,128)(2,1)S(1)} %get-tuple-element.17, bf16[1,16,4,8,128]{4,3,2,1,0:T(8,128)(2,1)} %get-tuple-element.22), kind=kOutput, calls=%fused_computation.4 | convolution fusion | flops 270532096 | bytes 6424576 | tf_op jit(solution)/shard_map/pkgh,tkh->kpgt/dot_general | solution.py:24
  46.7 3.3 %multiply_reduce_fusion.1 = (f32[4,16,8]{2,1,0:T(8,128)}, f32[4,16,8,2048]{3,2,1,0:T(8,128)}) fusion(bf16[1,2048,4,128]{3,2,1,0:T(4,128)(2,1)S(1)} %get-tuple-element.17, bf16[1,16,4,8,128]{4,3,2,1,0:T(8,128)(2,1)S(1)} %copy-done.10), kind=kOutput, calls=%fused_computation.5 | convolution fusion | flops 270532096 | bytes 6424576 | tf_op jit(solution)/shard_map/pkgh,tkh->kpgt/dot_general | solution.py:24
  50.0 3.3 %multiply_reduce_fusion.2 = (f32[4,16,8]{2,1,0:T(8,128)}, f32[4,16,8,2048]{3,2,1,0:T(8,128)}) fusion(bf16[1,2048,4,128]{3,2,1,0:T(4,128)(2,1)S(1)} %get-tuple-element.17, bf16[1,16,4,8,128]{4,3,2,1,0:T(8,128)(2,1)S(1)} %copy-done.9), kind=kOutput, calls=%fused_computation.6 | convolution fusion | flops 270532096 | bytes 6424576 | tf_op jit(solution)/shard_map/pkgh,tkh->kpgt/dot_general | solution.py:24
  53.5 2.7 %multiply_reduce_fusion.3 = (f32[4,16,8]{2,1,0:T(8,128)S(1)}, f32[4,16,8,2048]{3,2,1,0:T(8,128)}) fusion(bf16[1,2048,4,128]{3,2,1,0:T(4,128)(2,1)S(1)} %get-tuple-element.17, bf16[1,16,4,8,128]{4,3,2,1,0:T(8,128)(2,1)S(1)} %copy-done.8), kind=kOutput, calls=%fused_computation.7 | convolution fusion | flops 270532096 | bytes 6424576 | tf_op jit(solution)/shard_map/pkgh,tkh->kpgt/dot_general | solution.py:24
  56.2 1.1 copy_select_fusion
  57.3 1.6 fusion.102
  58.9 1.4 bitcast_maximum_fusion
  60.3 0.9 fusion.103
  61.2 0.6 bitcast_maximum_fusion.1
  62.1 0.3 fusion.104
  62.3 0.6 bitcast_maximum_fusion.2
  62.9 0.3 fusion.105
  63.2 22.3 %all-reduce.2 = (f32[16,4,8]{2,0,1:T(8,128)S(1)}, f32[16,4,8]{2,0,1:T(8,128)S(1)}, f32[16,4,8]{2,0,1:T(8,128)S(1)}, f32[16,4,8]{2,0,1:T(8,128)S(1)}) all-reduce(f32[16,4,8]{2,0,1:T(8,128)} %bitcast_maximum_fusion, f32[16,4,8]{2,0,1:T(8,128)} %bitcast_maximum_fusion.1, ...), channel_id=1, replica_groups=mesh['groups'=2,'ctx'=4,'dom'=2,'tp'=2] {'ctx'}, use_global_device_ids=true, to_apply=%region_27.28 | all-reduce | flops 2048 | bytes 16384 | tf_op jit(solution)/shard_map/pmax | solution.py:37
  85.6 1.0 fusion.66
  86.7 3.4 %fusion.41 = f32[16,4,8,128]{3,2,0,1:T(8,128)S(1)} fusion(bf16[1,2048,4,128]{3,2,1,0:T(4,128)(2,1)S(1)} %copy-done.6, f32[4,16,8,2048]{3,2,1,0:T(8,128)} %get-tuple-element.58, f32[4,16,8]{2,1,0:T(8,128)S(1)} %bitcast.214), kind=kOutput, calls=%fused_computation.49 | convolution fusion | flops 271581184 | bytes 6555648 | tf_op jit(solution)/shard_map/kpgt,tkh->pkgh/dot_general | solution.py:43
  90.1 1.0 convolution_add_fusion
  91.1 1.1 fusion.38
  92.3 1.0 convolution_add_fusion.1
  93.3 1.1 fusion.35
  94.5 1.0 convolution_add_fusion.2
  95.5 1.1 fusion.32
  96.7 1.0 convolution_add_fusion.3
  97.8 3.2 %fusion.6 = f32[4,16,8]{2,1,0:T(8,128)S(1)} fusion(f32[4,16,8,2048]{3,2,1,0:T(8,128)} %get-tuple-element.58, f32[4,16,8]{2,1,0:T(8,128)S(1)} %bitcast.215), kind=kLoop, calls=%fused_computation.14 | loop fusion | flops 3145216 | bytes 4198400 | tf_op jit(solution)/shard_map/reduce_sum | solution.py:40
  100.9 0.3 copy-done.3
  101.2 0.8 fusion.4
  102.0 0.6 copy-done.5
  102.7 0.8 fusion.2
  103.5 0.5 copy-done.1
  104.0 0.8 fusion
  104.9 21.4 %all-reduce = (f32[16,4,8]{2,0,1:T(8,128)S(1)}, f32[16,4,8]{2,0,1:T(8,128)S(1)}, f32[16,4,8]{2,0,1:T(8,128)S(1)}, f32[16,4,8]{2,0,1:T(8,128)S(1)}) all-reduce(f32[16,4,8]{2,0,1:T(8,128)S(1)} %bitcast_add_fusion, f32[16,4,8]{2,0,1:T(8,128)S(1)} %bitcast_add_fusion.1, ...), channel_id=1, replica_groups=mesh['groups'=2,'ctx'=4,'dom'=2,'tp'=2] {'ctx'}, use_global_device_ids=true, to_apply=%region_31.32 | all-reduce | flops 2048 | bytes 16384 | tf_op jit(solution)/shard_map/psum | solution.py:49
  126.3 25.9 %all-reduce.5.cloned.1.call-done = (f32[16,4,8,128]{3,2,0,1:T(8,128)}, f32[16,4,8,128]{3,2,0,1:T(8,128)}, f32[16,4,8,128]{3,2,0,1:T(8,128)}, f32[16,4,8,128]{3,2,0,1:T(8,128)}) async-done(((f32[16,4,8,128]{3,2,0,1:T(8,128)}, f32[16,4,8,128]{3,2,0,1:T(8,128)}, f32[16,4,8,128]{3,2,0,1:T(8,128)}, f32[16,4,8,128]{3,2,0,1:T(8,128)}), (f32[16,4,8,128]{3,2,0,1:T(8,128)}, f32[16,4,8,128]{3,2,0,1:T(8,128)}, ...) | async-done | bytes 1048592 | tf_op jit(solution)/shard_map/psum | solution.py:49
  152.3 1.1 fusion.59
  153.4 1.1 fusion.58
  154.4 1.1 fusion.57
  155.5 1.1 fusion.56
  156.7 0.9 copy.130
  (91 shorter events, 4.0 us)
Async XLA Ops:
  6.5 145.7 %all-reduce.5.cloned.1.call-start = ((), (), s32[]{:S(2)}) async-start(), calls=%async_computation | async-start | bytes 2097152 | tf_op jit(solution)/shard_map/psum | solution.py:49
  8.8 4.1 %copy-start.7 = (bf16[4,16,4,8,128]{4,3,2,1,0:T(8,128)(2,1)S(1)}, bf16[4,16,4,8,128]{4,3,2,1,0:T(8,128)(2,1)}, u32[]{:S(2)}) copy-start(bf16[4,16,4,8,128]{4,3,2,1,0:T(8,128)(2,1)} %param.6) | copy-start | bytes 1572868
  8.8 4.9 %copy-start.18 = (bf16[4,2,16,4,128]{4,3,2,1,0:T(4,128)(2,1)S(1)}, bf16[4,2,16,4,128]{4,3,2,1,0:T(4,128)(2,1)}, u32[]{:S(2)}) copy-start(bf16[4,2,16,4,128]{4,3,2,1,0:T(4,128)(2,1)} %param.9) | copy-start | bytes 393220
  8.8 8.1 %copy-start.19 = (bf16[2,16,4,4,128]{4,3,2,1,0:T(4,128)(2,1)S(1)}, bf16[2,16,4,4,128]{4,3,2,1,0:T(4,128)(2,1)}, u32[]{:S(2)}) copy-start(bf16[2,16,4,4,128]{4,3,2,1,0:T(4,128)(2,1)} %param.8) | copy-start | bytes 393220
  14.4 0.6 copy-start.15
  14.4 2.2 %copy-start.11 = (bf16[2,16,4,128]{3,2,1,0:T(4,128)(2,1)}, bf16[2,16,4,128]{3,2,1,0:T(4,128)(2,1)S(1)}, u32[]{:S(2)}) copy-start(bf16[2,16,4,128]{3,2,1,0:T(4,128)(2,1)S(1)} %get-tuple-element.32) | copy-start | bytes 98308
  14.4 2.2 %copy-start.13 = (bf16[2,16,4,128]{3,2,1,0:T(4,128)(2,1)}, bf16[2,16,4,128]{3,2,1,0:T(4,128)(2,1)S(1)}, u32[]{:S(2)}) copy-start(bf16[2,16,4,128]{3,2,1,0:T(4,128)(2,1)S(1)} %get-tuple-element.33) | copy-start | bytes 98308
  36.3 10.4 %copy-start.10 = (bf16[1,16,4,8,128]{4,3,2,1,0:T(8,128)(2,1)S(1)}, bf16[1,16,4,8,128]{4,3,2,1,0:T(8,128)(2,1)}, u32[]{:S(2)}) copy-start(bf16[1,16,4,8,128]{4,3,2,1,0:T(8,128)(2,1)} %get-tuple-element.20) | copy-start | bytes 393220
  46.7 3.3 %copy-start.9 = (bf16[1,16,4,8,128]{4,3,2,1,0:T(8,128)(2,1)S(1)}, bf16[1,16,4,8,128]{4,3,2,1,0:T(8,128)(2,1)}, u32[]{:S(2)}) copy-start(bf16[1,16,4,8,128]{4,3,2,1,0:T(8,128)(2,1)} %get-tuple-element.21) | copy-start | bytes 393220
  50.0 3.5 %copy-start.8 = (bf16[1,16,4,8,128]{4,3,2,1,0:T(8,128)(2,1)S(1)}, bf16[1,16,4,8,128]{4,3,2,1,0:T(8,128)(2,1)}, u32[]{:S(2)}) copy-start(bf16[1,16,4,8,128]{4,3,2,1,0:T(8,128)(2,1)} %get-tuple-element.19) | copy-start | bytes 393220
  53.4 7.8 %copy-start.17 = (f32[4,16,8]{2,1,0:T(8,128)S(1)}, f32[4,16,8]{2,1,0:T(8,128)}, u32[]{:S(2)}) copy-start(f32[4,16,8]{2,1,0:T(8,128)} %get-tuple-element.67) | copy-start | bytes 6148
  53.5 8.4 %copy-start.12 = (bf16[2,16,4,128]{3,2,1,0:T(4,128)(2,1)S(1)}, bf16[2,16,4,128]{3,2,1,0:T(4,128)(2,1)}, u32[]{:S(2)}) copy-start(bf16[2,16,4,128]{3,2,1,0:T(4,128)(2,1)} %copy-done.11) | copy-start | bytes 98308
  53.5 8.4 %copy-start.14 = (bf16[2,16,4,128]{3,2,1,0:T(4,128)(2,1)S(1)}, bf16[2,16,4,128]{3,2,1,0:T(4,128)(2,1)}, u32[]{:S(2)}) copy-start(bf16[2,16,4,128]{3,2,1,0:T(4,128)(2,1)} %copy-done.13) | copy-start | bytes 98308
  53.5 8.6 %copy-start.21 = (pred[16,4]{1,0:T(8,128)(4,1)S(1)}, pred[16,4]{1,0:T(8,128)(4,1)}, u32[]{:S(2)}) copy-start(pred[16,4]{1,0:T(8,128)(4,1)} %get-tuple-element.52) | copy-start | bytes 196
  53.5 8.8 %copy-start.16 = (f32[4,16,8]{2,1,0:T(8,128)S(1)}, f32[4,16,8]{2,1,0:T(8,128)}, u32[]{:S(2)}) copy-start(f32[4,16,8]{2,1,0:T(8,128)} %get-tuple-element.71) | copy-start | bytes 6148
  53.5 9.4 %copy-start.20 = (pred[16,4]{1,0:T(8,128)(4,1)S(1)}, pred[16,4]{1,0:T(8,128)(4,1)}, u32[]{:S(2)}) copy-start(pred[16,4]{1,0:T(8,128)(4,1)} %get-tuple-element.43) | copy-start | bytes 196
  56.2 30.5 %copy-start.6 = (bf16[1,2048,4,128]{3,2,1,0:T(4,128)(2,1)S(1)}, bf16[1,2048,4,128]{3,2,1,0:T(4,128)(2,1)}, u32[]{:S(2)}) copy-start(bf16[1,2048,4,128]{3,2,1,0:T(4,128)(2,1)} %get-tuple-element.18) | copy-start | bytes 6291460
  86.7 4.4 %copy-start.2 = (f32[4,16,8,2048]{3,2,1,0:T(8,128)S(1)}, f32[4,16,8,2048]{3,2,1,0:T(8,128)}, u32[]{:S(2)}) copy-start(f32[4,16,8,2048]{3,2,1,0:T(8,128)} %get-tuple-element.68) | copy-start | bytes 12582916
  91.1 2.2 %copy-start.4 = (f32[4,16,8,2048]{3,2,1,0:T(8,128)S(1)}, f32[4,16,8,2048]{3,2,1,0:T(8,128)}, u32[]{:S(2)}) copy-start(f32[4,16,8,2048]{3,2,1,0:T(8,128)} %get-tuple-element.72) | copy-start | bytes 12582916
  93.3 2.2 %copy-start = (f32[4,16,8,2048]{3,2,1,0:T(8,128)S(1)}, f32[4,16,8,2048]{3,2,1,0:T(8,128)}, u32[]{:S(2)}) copy-start(f32[4,16,8,2048]{3,2,1,0:T(8,128)} %get-tuple-element.76) | copy-start | bytes 12582916
  97.7 3.5 %copy-start.3 = (f32[4,16,8,2048]{3,2,1,0:T(8,128)S(1)}, f32[4,16,8,2048]{3,2,1,0:T(8,128)}, u32[]{:S(2)}) copy-start(f32[4,16,8,2048]{3,2,1,0:T(8,128)} %get-tuple-element.68) | copy-start | bytes 12582916
  97.8 4.9 %copy-start.5 = (f32[4,16,8,2048]{3,2,1,0:T(8,128)S(1)}, f32[4,16,8,2048]{3,2,1,0:T(8,128)}, u32[]{:S(2)}) copy-start(f32[4,16,8,2048]{3,2,1,0:T(8,128)} %get-tuple-element.72) | copy-start | bytes 12582916
  101.2 2.8 %copy-start.1 = (f32[4,16,8,2048]{3,2,1,0:T(8,128)S(1)}, f32[4,16,8,2048]{3,2,1,0:T(8,128)}, u32[]{:S(2)}) copy-start(f32[4,16,8,2048]{3,2,1,0:T(8,128)} %get-tuple-element.76) | copy-start | bytes 12582916
Sparse Core Ops, SparseCore 0:
  97.9 54.3 all-reduce.4
where the time goes:
time: 165 us; the launch traced here: 164 us
  blocking collectives  67.9 us (41%)
  matrix products  27.9 us (17%)
  waiting for transfers between devices  26 us (16%)
  other arithmetic  17.6 us (11%)
  between operations  13.9 us (8%)
  local copies, waits for them, and re-layouts  11.3 us (7%)
    psum x1, waiting for transfers between devices, attend(): total_all, numerator_all = lax.psum((totals, numerator), 'ctx')  25.9 us
    all_gather x4, blocking collectives, resample_whole(): lax.all_gather(flat_rows, 'dom', axis=1, tiled=True)  24.2 us
    pmax x1, blocking collectives, attend(): peak_score = lax.pmax(local_peak, 'ctx')  22.3 us
    psum x1, blocking collectives, attend(): total_all, numerator_all = lax.psum((totals, numerator), 'ctx')  21.4 us
    dot_general x4, matrix products, attend(): jnp.einsum('pkgh,tkh->kpgt', query_block, prompt_keys, preferred_element_...  13.4 us
    dot_general x4, matrix products, attend(): jnp.einsum('kpgt,tkh->pkgh', prompt_weights, prompt_values, preferred_ele...  6.59 us
    reduce_sum x4, other arithmetic, attend(): jnp.sum(prompt_exp, axis=-1)  5.62 us
    another operation x5, other arithmetic, on_device(): return jnp.stack(results)  4.42 us
  transfers between devices with their start and end apart: 1, of which 1 were waited for; matrix products, arithmetic and copies ran while one was open for 3% of the time, Pallas kernels for 0%

commit v1 on v0

v1 whole, which is shorter than its diff:
```python
import functools
import math

import jax
import jax.numpy as jnp
from jax import lax
from jax.experimental import pallas as pl
from jax.experimental.pallas import tpu as pltpu
from jax.sharding import PartitionSpec as P

LANES = 128
HIDDEN = -1e30
NN = (((1,), (0,)), ((), ()))
NT = (((1,), (1,)), ((), ()))


def round_up(value, multiple):
    return -(-value // multiple) * multiple


def dot(a, b, dims):
    return lax.dot_general(a, b, dims, preferred_element_type=jnp.float32)


def eye_mask(rows):
    shape = (rows, LANES)
    return lax.broadcasted_iota(jnp.int32, shape, 0) == lax.broadcasted_iota(jnp.int32, shape, 1)


def column_to_lanes(column):
    rows = column.shape[0]
    block = min(rows, LANES)
    mask = eye_mask(block)
    return jnp.concatenate(
        [
            jnp.sum(jnp.where(mask, column[at : at + block], 0.0), axis=0, keepdims=True)
            for at in range(0, rows, block)
        ],
        axis=0,
    )


def lanes_to_column(lanes, rows):
    block = min(rows, LANES)
    mask = eye_mask(block)
    return jnp.concatenate(
        [
            jnp.sum(jnp.where(mask, lanes[i : i + 1], 0.0), axis=1, keepdims=True)
            for i in range(lanes.shape[0])
        ],
        axis=0,
    )


def tail_rows(rows):
    return round_up(3 * -(-rows // LANES), 16)


def pack_tail(column):
    lanes = column_to_lanes(column)
    high = lanes.astype(jnp.bfloat16).astype(jnp.float32)
    middle = (lanes - high).astype(jnp.bfloat16).astype(jnp.float32)
    low = lanes - high - middle
    parts = jnp.concatenate([high, middle, low], axis=0)
    spare = tail_rows(column.shape[0]) - parts.shape[0]
    return jnp.concatenate([parts, jnp.zeros((spare, LANES), jnp.float32)], axis=0).astype(
        jnp.bfloat16
    )


def unpack_tail(tail, rows):
    tail = tail.astype(jnp.float32)
    blocks = -(-rows // LANES)
    lanes = tail[:blocks] + tail[blocks : 2 * blocks] + tail[2 * blocks : 3 * blocks]
    return lanes_to_column(lanes, rows)


def split_heads_kernel(heads, rows_ref, out_ref, wide):
    wide[...] = rows_ref[0].astype(jnp.float32)
    steps = out_ref.shape[2]
    for head in range(heads):
        out_ref[0, head] = wide[pl.ds(head, steps, stride=heads), :].astype(out_ref.dtype)


def split_heads(rows, heads):
    total = rows.shape[1] // heads
    block = math.gcd(total, 512)
    size = rows.shape[2]
    return pl.pallas_call(
        functools.partial(split_heads_kernel, heads),
        grid=(2, total // block),
        in_specs=[pl.BlockSpec((1, block * heads, size), lambda kind, at: (kind, at, 0))],
        out_specs=pl.BlockSpec((1, heads, block, size), lambda kind, at: (kind, 0, at, 0)),
        out_shape=jax.ShapeDtypeStruct((2, heads, total, size), rows.dtype),
        scratch_shapes=[pltpu.VMEM((block * heads, size), jnp.float32)],
        compiler_params=pltpu.CompilerParams(vmem_limit_bytes=16 << 20),
        cost_estimate=pl.CostEstimate(
            flops=0, bytes_accessed=4 * rows.size, transcendentals=0
        ),
    )(rows)


def suffix_kernel(
    heads, per_owner, suffix_dev, tokens_dev, *refs
):
    *row_refs, ancestors_ref, lengths_ref, keys_ref, bias_ref, wide = refs
    owners = len(row_refs)
    particles = owners * per_owner
    steps = ancestors_ref.shape[0]
    slots = suffix_dev + tokens_dev
    columns = owners * per_owner * slots
    padded = keys_ref.shape[2]
    my_owner = lax.axis_index("dom")
    my_shard = lax.axis_index("ctx")
    each = per_owner * slots
    for kind in range(2):
        for at, ref in enumerate(row_refs):
            wide[pl.ds(at * each * heads, each * heads), :] = ref[kind].astype(jnp.float32)
        for head in range(heads):
            pieces = [wide[pl.ds(head, columns, stride=heads), :]]
            if padded > columns:
                pieces.append(jnp.zeros((padded - columns, LANES), jnp.float32))
            keys_ref[kind, head] = jnp.concatenate(pieces, axis=0).astype(keys_ref.dtype)

    def iota(shape, axis):
        return lax.broadcasted_iota(jnp.int32, shape, axis)

    square = (particles, particles)
    same = iota(square, 0) == iota(square, 1)

    def as_column(row):
        return jnp.sum(jnp.where(same, row, 0), axis=1, keepdims=True)

    unit = same.astype(jnp.float32)
    state = jnp.concatenate([unit, jnp.zeros((particles, tokens_dev * particles), jnp.float32)], axis=1)
    pick = (iota((per_owner, particles), 1) == iota((per_owner, particles), 0) + my_owner * per_owner)
    pick = pick.astype(jnp.bfloat16)
    mine = []
    for step in range(steps):
        parent = as_column(ancestors_ref[step : step + 1, :])
        move = (parent == iota(square, 1)).astype(jnp.bfloat16)
        state = dot(move, state.astype(jnp.bfloat16), NN)
        blocks = [state[:, :particles]]
        for token in range(tokens_dev):
            written = my_shard * tokens_dev + token
            old = state[:, (1 + token) * particles : (2 + token) * particles]
            blocks.append(jnp.where(written == step, unit, old))
        state = jnp.concatenate(blocks, axis=1)
        mine.append(dot(pick, state.astype(jnp.bfloat16), NN))
    mine = jnp.concatenate(mine, axis=0).astype(jnp.bfloat16)
    lengths = as_column(lengths_ref[...])
    column = iota((particles, padded), 1)
    source = column // each
    owner = lax.rem(my_owner + owners - source, owners)
    inner = column - source * each
    particle = owner * per_owner + inner // slots
    slot = lax.rem(inner, slots)
    here = (iota((particles, padded), 0) == particle) & (column < columns)
    position = my_shard * suffix_dev + slot
    seen = [here & (slot < suffix_dev) & (position < lengths)]
    seen += [here & (slot == suffix_dev + token) for token in range(tokens_dev)]
    table = jnp.concatenate([s.astype(jnp.bfloat16) for s in seen], axis=0)
    bias_ref[...] = jnp.where(dot(mine, table, NN) > 0.5, 0.0, HIDDEN)


def suffix_part(row_list, ancestors, lengths, heads, suffix_dev, tokens_dev):
    per_owner = row_list[0].shape[1] // (heads * (suffix_dev + tokens_dev))
    columns = len(row_list) * row_list[0].shape[1] // heads
    padded = round_up(columns, LANES)
    size = row_list[0].shape[2]
    steps = ancestors.shape[0]
    return pl.pallas_call(
        functools.partial(suffix_kernel, heads, per_owner, suffix_dev, tokens_dev),
        out_shape=(
            jax.ShapeDtypeStruct((2, heads, padded, size), jnp.bfloat16),
            jax.ShapeDtypeStruct((steps * per_owner, padded), jnp.float32),
        ),
        scratch_shapes=[pltpu.VMEM((columns * heads, size), jnp.float32)],
        compiler_params=pltpu.CompilerParams(vmem_limit_bytes=24 << 20),
        cost_estimate=pl.CostEstimate(flops=0, bytes_accessed=1 << 20, transcendentals=0),
    )(*row_list, ancestors, lengths.reshape(1, -1))


def attend_kernel(scale, q_ref, k_ref, v_ref, kx_ref, vx_ref, bias_ref, send_ref, keep_ref, sums_ref):
    steps, per_owner, _, group, size = q_ref.shape
    half = steps * per_owner // 2
    rows = half * group
    columns = bias_ref.shape[1]
    bit = lax.rem(lax.axis_index("ctx"), 2)
    factor = scale * math.log2(math.e)

    def one_half(which):
        q = q_ref[pl.ds(which * (steps // 2), steps // 2)].reshape(rows, size)
        bias = bias_ref[pl.ds(pl.multiple_of(which * half, half), half), :]
        bias = jnp.broadcast_to(bias[:, None, :], (half, group, columns)).reshape(rows, columns)
        scores = dot(q, k_ref[0, 0], NT)
        extra = dot(q, kx_ref[0, 0], NT) + bias
        peak = jnp.maximum(
            jnp.max(scores, axis=1, keepdims=True), jnp.max(extra, axis=1, keepdims=True)
        )
        offset = peak * factor
        weight = jnp.exp2(scores * factor - offset).astype(jnp.bfloat16)
        weight_extra = jnp.exp2(extra * factor - offset).astype(jnp.bfloat16)

        def with_ones(values):
            return jnp.concatenate([values, jnp.ones_like(values)], axis=1)

        total = dot(weight, with_ones(v_ref[0, 0]), NN) + dot(
            weight_extra, with_ones(vx_ref[0, 0]), NN
        )
        sums = total[:, size:]
        return total[:, :size] / sums, offset + jnp.log2(sums[:, :1])

    out, log_sum = one_half(1 - bit)
    send_ref[0, :rows] = out.astype(jnp.bfloat16)
    send_ref[0, rows:] = pack_tail(log_sum)
    out, log_sum = one_half(bit)
    keep_ref[0] = out
    sums_ref[0] = jnp.broadcast_to(log_sum, sums_ref.shape[1:])


def attend(queries, prompt, extra, bias, head, count, scale):
    steps, per_owner, _, group, size = queries.shape
    total = prompt.shape[2]
    padded = extra.shape[2]
    rows = steps * per_owner * group // 2
    message = rows + tail_rows(rows)

    def kind_spec(length, kind):
        return pl.BlockSpec((1, 1, length, size), lambda i: (kind, head + i, 0, 0))

    return pl.pallas_call(
        functools.partial(attend_kernel, scale),
        grid=(count,),
        in_specs=[
            pl.BlockSpec((steps, per_owner, 1, group, size), lambda i: (0, 0, head + i, 0, 0)),
            kind_spec(total, 0),
            kind_spec(total, 1),
            kind_spec(padded, 0),
            kind_spec(padded, 1),
            pl.BlockSpec(bias.shape, lambda i: (0, 0)),
        ],
        out_specs=[
            pl.BlockSpec((1, message, size), lambda i: (i, 0, 0)),
            pl.BlockSpec((1, rows, size), lambda i: (i, 0, 0)),
            pl.BlockSpec((1, rows, LANES), lambda i: (i, 0, 0)),
        ],
        out_shape=(
            jax.ShapeDtypeStruct((count, message, size), jnp.bfloat16),
            jax.ShapeDtypeStruct((count, rows, size), jnp.float32),
            jax.ShapeDtypeStruct((count, rows, LANES), jnp.float32),
        ),
        compiler_params=pltpu.CompilerParams(vmem_limit_bytes=40 << 20),
        cost_estimate=pl.CostEstimate(
            flops=count * 8 * rows * (total + padded) * size,
            bytes_accessed=count * 4 * total * size,
            transcendentals=count * 2 * rows * (total + padded),
        ),
    )(queries, prompt, prompt, extra, extra, bias)


def merge(out_a, sum_a, out_b, sum_b):
    top = jnp.maximum(sum_a, sum_b)
    weight_a = jnp.exp2(sum_a - top)
    weight_b = jnp.exp2(sum_b - top)
    total = weight_a + weight_b
    return (out_a * weight_a + out_b * weight_b) / total, top + jnp.log2(total)


def merge_kernel(level, last, keep_ref, sums_ref, got_ref, *outs):
    rows = keep_ref.shape[1]
    for i in range(keep_ref.shape[0]):
        got_sum = unpack_tail(got_ref[i, rows:], rows)
        out, log_sum = merge(
            keep_ref[i], sums_ref[i][:, :1], got_ref[i, :rows].astype(jnp.float32), got_sum
        )
        if last:
            outs[0][i, :rows] = out.astype(jnp.bfloat16)
            outs[0][i, rows:] = pack_tail(log_sum)
        else:
            half = rows // 2
            bit = lax.rem(lax.axis_index("ctx") >> level, 2) == 1
            send, keep, wide = outs

            def choose(first, value):
                return jnp.where(first, value[:half], value[half:])

            send[i, :half] = choose(bit, out).astype(jnp.bfloat16)
            send[i, half:] = pack_tail(choose(bit, log_sum))
            keep[i] = choose(~bit, out)
            wide[i] = jnp.broadcast_to(choose(~bit, log_sum), (half, LANES))


def merge_parts(keep, sums, got, level, last):
    count, rows, size = keep.shape
    part = rows if last else rows // 2
    shapes = [jax.ShapeDtypeStruct((count, part + tail_rows(part), size), jnp.bfloat16)]
    if not last:
        shapes.append(jax.ShapeDtypeStruct((count, part, size), jnp.float32))
        shapes.append(jax.ShapeDtypeStruct((count, part, LANES), jnp.float32))
    return pl.pallas_call(
        functools.partial(merge_kernel, level, last),
        out_shape=tuple(shapes),
        compiler_params=pltpu.CompilerParams(vmem_limit_bytes=16 << 20),
        cost_estimate=pl.CostEstimate(
            flops=8 * keep.size, bytes_accessed=8 * keep.size, transcendentals=0
        ),
    )(keep, sums, got)


def finish_kernel(mine_ref, got_ref, out_ref):
    rows = out_ref.shape[1]
    for i in range(mine_ref.shape[0]):
        out, _ = merge(
            mine_ref[i, :rows].astype(jnp.float32),
            unpack_tail(mine_ref[i, rows:], rows),
            got_ref[i, :rows].astype(jnp.float32),
            unpack_tail(got_ref[i, rows:], rows),
        )
        out_ref[i] = out.astype(jnp.bfloat16)


def finish(mine, got, rows):
    count, _, size = mine.shape
    return pl.pallas_call(
        finish_kernel,
        out_shape=jax.ShapeDtypeStruct((count, rows, size), jnp.bfloat16),
        compiler_params=pltpu.CompilerParams(vmem_limit_bytes=16 << 20),
        cost_estimate=pl.CostEstimate(
            flops=8 * mine.size, bytes_accessed=6 * mine.size, transcendentals=0
        ),
    )(mine, got)


def place_kernel(chunks, *refs):
    *halves, out_ref = refs
    both, _, group, size = (out_ref.shape[0] * out_ref.shape[1],) + out_ref.shape[2:]
    steps, per_owner = out_ref.shape[:2]
    half = steps // 2
    bit = lax.rem(lax.axis_index("ctx"), 2)
    head = 0
    for chunk in range(chunks):
        own, other = halves[2 * chunk : 2 * chunk + 2]
        for i in range(own.shape[0]):
            shape = (half, per_owner, group, size)
            out_ref[pl.ds(bit * half, half), :, head] = own[i].reshape(shape)
            out_ref[pl.ds((1 - bit) * half, half), :, head] = other[i].reshape(shape)
            head += 1


def place(pairs, shape):
    flat = [half for pair in pairs for half in pair]
    return pl.pallas_call(
        functools.partial(place_kernel, len(pairs)),
        out_shape=jax.ShapeDtypeStruct(shape, jnp.bfloat16),
        compiler_params=pltpu.CompilerParams(vmem_limit_bytes=16 << 20),
        cost_estimate=pl.CostEstimate(flops=0, bytes_accessed=1 << 20, transcendentals=0),
    )(*flat)


def on_device(shards, owners, chunks, queries, prompt_cache, suffix_cache, new_kv, ancestors, lengths):
    steps, per_owner, heads, group, size = queries.shape
    suffix_dev = suffix_cache.shape[2]
    my_shard = lax.axis_index("ctx")
    scale = 1.0 / math.sqrt(size)
    levels = shards.bit_length() - 1

    def swap(value, bit):
        return lax.ppermute(value, "ctx", [(i, i ^ (1 << bit)) for i in range(shards)])

    tokens_dev = -(-steps // shards)
    first = jnp.minimum(my_shard * tokens_dev, steps - tokens_dev)
    tokens = lax.dynamic_slice_in_dim(new_kv, first, tokens_dev, axis=0)
    rows = jnp.concatenate([suffix_cache, jnp.moveaxis(tokens, 0, 2)], axis=2)
    rows = rows.reshape(2, -1, size)
    row_list = [rows] + [
        lax.ppermute(rows, "dom", [(i, (i + hop) % owners) for i in range(owners)])
        for hop in range(1, owners)
    ]
    prompt = split_heads(prompt_cache.reshape(2, -1, size), heads)
    extra, bias = suffix_part(row_list, ancestors, lengths, heads, suffix_dev, tokens_dev)

    each = heads // chunks
    pairs = []
    for chunk in range(chunks):
        send, keep, sums = attend(queries, prompt, extra, bias, chunk * each, each, scale)
        for level in range(1, levels):
            got = swap(send, level - 1)
            outs = merge_parts(keep, sums, got, level, level == levels - 1)
            if level == levels - 1:
                (send,) = outs
            else:
                send, keep, sums = outs
        part = steps * per_owner * group >> (levels - 1)
        done = finish(send, swap(send, levels - 1), part)
        for level in range(levels - 2, 0, -1):
            other = swap(done, level)
            flip = (my_shard >> level) % 2 == 1
            done = jnp.where(
                flip,
                jnp.concatenate([other, done], axis=1),
                jnp.concatenate([done, other], axis=1),
            )
        pairs.append((done, swap(done, 0)))
    return place(pairs, queries.shape)


def solution(mesh):
    return jax.shard_map(
        functools.partial(on_device, mesh.shape["ctx"], mesh.shape["dom"], 4),
        mesh=mesh,
        in_specs=(
            P("groups", "dom", "tp", None, None),
            P("groups", "ctx", "tp", None),
            P("groups", "dom", "ctx", "tp", None),
            P("groups", None, "dom", "tp", None),
            P("groups", None),
            P("groups"),
        ),
        out_specs=P("groups", "dom", "tp", None, None),
        check_vma=False,
    )
```

time: 165 us -> 44.8 us (0.27)
  blocking collectives: 67.9 us -> 0 us
  matrix products: 27.9 us -> 0 us
  waiting for transfers between devices: 26 us -> 6.13 us
  starting transfers between devices: 0.01 us -> 18.7 us
  other arithmetic: 17.6 us -> 1.02 us
  Pallas kernels: 0 us -> 15.5 us
  between operations: 13.9 us -> 0.07 us
  local copies, waits for them, and re-layouts: 11.3 us -> 3.12 us
    dot_general x20 -> x0, matrix products: 27.9 us -> none  [the longest x4 13.4 us: attend(): jnp.einsum('pkgh,tkh->kpgt', query_block, prompt_keys, preferred_element_...]
    psum x1 -> x0, waiting for transfers between devices: 25.9 us -> none  [attend(): total_all, numerator_all = lax.psum((totals, numerator), 'ctx')]
    all_gather x4 -> x0, blocking collectives: 24.2 us -> none  [resample_whole(): lax.all_gather(flat_rows, 'dom', axis=1, tiled=True)]
    pmax x1 -> x0, blocking collectives: 22.3 us -> none  [attend(): peak_score = lax.pmax(local_peak, 'ctx')]
    psum x1 -> x0, blocking collectives: 21.4 us -> none  [attend(): total_all, numerator_all = lax.psum((totals, numerator), 'ctx')]
    ppermute x0 -> x13, starting transfers between devices: none -> 18.7 us  [the longest x12 15.7 us: swap(): lax.ppermute(value, 'ctx', [(i, i ^ 1 << bit) for i in range(shards)])]
    pallas_call x0 -> x15, Pallas kernels: none -> 15.5 us  [the longest x4 9.14 us: attend(): pl.pallas_call(functools.partial(attend_kernel, scale), grid=(count,), in...]
    reduce_sum x12 -> x0, other arithmetic: 8.47 us -> none  [the longest x4 5.62 us: attend(): jnp.sum(prompt_exp, axis=-1)]
  transfers between devices with their start and end apart: 1 -> 13, of which waited for: 1 -> 6; matrix products, arithmetic and copies ran while one was open for 3% -> 0% of each run, Pallas kernels for 0% -> 14%
where the time goes in v1:
time: 44.8 us; the launch traced here: 44.6 us
  starting transfers between devices  18.7 us (42%)
  Pallas kernels  15.5 us (35%)
  waiting for transfers between devices  6.13 us (14%)
  local copies, waits for them, and re-layouts  3.12 us (7%)
  other arithmetic  1.02 us (2%)
    ppermute x12, starting transfers between devices, swap(): lax.ppermute(value, 'ctx', [(i, i ^ 1 << bit) for i in range(shards)])  15.7 us
    pallas_call x4, Pallas kernels, attend(): pl.pallas_call(functools.partial(attend_kernel, scale), grid=(count,), in...  9.14 us
    ppermute x12, waiting for transfers between devices, swap(): lax.ppermute(value, 'ctx', [(i, i ^ 1 << bit) for i in range(shards)])  5.61 us
    unnamed x10, local copies, waits for them, and re-layouts  3.1 us
    ppermute x1, starting transfers between devices, on_device(): lax.ppermute(rows, 'dom', [(i, (i + hop) % owners) for i in range(owners)])  3 us
    pallas_call x1, Pallas kernels, split_heads(): pl.pallas_call(functools.partial(split_heads_kernel, heads), grid=(2, tot...  1.47 us
    pallas_call x1, Pallas kernels, suffix_part(): pl.pallas_call(functools.partial(suffix_kernel, heads, per_owner, suffix_...  1.38 us
    pallas_call x4, Pallas kernels, finish(): pl.pallas_call(finish_kernel, out_shape=jax.ShapeDtypeStruct((count, rows...  1.32 us
  transfers between devices with their start and end apart: 13, of which 6 were waited for; matrix products, arithmetic and copies ran while one was open for 0% of the time, Pallas kernels for 14%

profile of v1, /device:TPU:0, one launch (start us, length us, event | category | flops | bytes accessed | tf_op | source)
XLA Modules:
  0.0 44.6 jit_solution(15728294090423853797)
XLA Ops:
  0.0 0.0 copy-start
  0.0 0.9 %copy-done = bf16[4,2,16,4,128]{4,3,2,1,0:T(4,128)(2,1)S(1)} copy-done((bf16[4,2,16,4,128]{4,3,2,1,0:T(4,128)(2,1)S(1)}, bf16[4,2,16,4,128]{4,3,2,1,0:T(4,128)(2,1)}, u32[]{:S(2)}) %copy-start) | copy-done | bytes 131096
  0.9 1.0 %pad_maximum_fusion = bf16[2,16,5,4,128]{4,3,2,1,0:T(4,128)(2,1)S(1)} fusion(bf16[2,16,1,4,128]{4,3,2,1,0:T(4,128)(2,1)S(1)} %dynamic-slice_bitcast_fusion, bf16[2,16,4,4,128]{4,3,2,1,0:T(4,128)(2,1)} %param.8), kind=kLoop, calls=%fused_computation | loop fusion | flops 81920 | bytes 327680 | tf_op jit(solution)/shard_map/concatenate | solution.py:374
  1.9 3.0 %collective-permute-start = (bf16[2,320,128]{2,1,0:T(8,128)(2,1)S(1)}, bf16[2,320,128]{2,1,0:T(8,128)(2,1)S(1)}, u32[]{:S(2)}, u32[]{:S(2)}) collective-permute-start(bf16[2,320,128]{2,1,0:T(8,128)(2,1)S(1)} %bitcast.6), channel_id=1, source_target_pairs={{0,2},{2,0},{1,3},{3,1},{4,6},{6,4},{5,7},{7,5},{8,10},{10,8},{9,1... | collective-permute-start | bytes 491528 | tf_op jit(solution)/shard_map/ppermute | solution.py:377
  5.0 2.2 %copy-done.2 = bf16[2,2048,4,128]{3,2,1,0:T(4,128)(2,1)S(1)} copy-done((bf16[2,2048,4,128]{3,2,1,0:T(4,128)(2,1)S(1)}, bf16[2,2048,4,128]{3,2,1,0:T(4,128)(2,1)}, u32[]{:S(2)}) %copy-start.2) | copy-done | bytes 4194328
  7.1 1.5 %shard_map.64.k_ref.v_ref = bf16[2,4,2048,128]{3,2,1,0:T(8,128)(2,1)S(1)} custom-call(bf16[2,8192,128]{2,1,0:T(8,128)(2,1)S(1)} %bitcast.5), custom_call_target="tpu_custom_call" | custom-call | bytes 8388608 | tf_op jit(solution)/shard_map/pallas_call | solution.py:89
  8.6 0.5 %collective-permute-done.refs_1_ = bf16[2,320,128]{2,1,0:T(8,128)(2,1)S(1)} collective-permute-done((bf16[2,320,128]{2,1,0:T(8,128)(2,1)S(1)}, bf16[2,320,128]{2,1,0:T(8,128)(2,1)S(1)}, u32[]{:S(2)}, u32[]{:S(2)}) %collective-permute-start) | collective-permute-done | bytes 163872 | tf_op jit(solution)/shard_map/ppermute | solution.py:377
  9.2 0.0 copy-done.3
  9.2 0.0 copy-done.4
  9.2 1.4 %shard_map.65 = (bf16[2,4,256,128]{3,2,1,0:T(8,128)(2,1)S(1)}, f32[64,256]{1,0:T(8,128)S(1)}) custom-call(bf16[2,320,128]{2,1,0:T(8,128)(2,1)S(1)} %bitcast.7, bf16[2,320,128]{2,1,0:T(8,128)(2,1)S(1)} %collective-permute-done.refs_1_, s32[4,32]{1,0:T(4,128)S(1)} %copy-done.3, s32[1,32]{1,0:T(1,128)S(1)} %bitcast.8), custom_call_target="tpu_custom_call" | custom-call | bytes 1048576 | tf_op jit(solution)/shard_map/pallas_call | solution.py:172
  10.5 0.0 copy-done.1
  10.5 2.3 %shard_map.75 = (bf16[1,272,128]{2,1,0:T(8,128)(2,1)S(1)}, f32[1,256,128]{2,1,0:T(8,128)S(1)}, f32[1,256,128]{2,1,0:T(8,128)S(1)}) custom-call(bf16[4,16,4,8,128]{4,3,2,1,0:T(8,128)(2,1)S(1)} %copy-done.1, bf16[2,4,2048,128]{3,2,1,0:T(8,128)(2,1)S(1)} %shard_map.64.k_ref.v_ref, bf16[2,4,2048,128]{3,2,1,0:T(8,128)(2,1)S(1)} %shard_map.64.k_ref.v_ref, ...), custom_call_target="tpu_custom_call" | custom-call | flops 603979776 | bytes 1048576 | tf_op jit(solution)/shard_map/pallas_call | solution.py:232
  12.8 2.3 %shard_map.72 = (bf16[1,272,128]{2,1,0:T(8,128)(2,1)S(1)}, f32[1,256,128]{2,1,0:T(8,128)S(1)}, f32[1,256,128]{2,1,0:T(8,128)S(1)}) custom-call(bf16[4,16,4,8,128]{4,3,2,1,0:T(8,128)(2,1)S(1)} %copy-done.1, bf16[2,4,2048,128]{3,2,1,0:T(8,128)(2,1)S(1)} %shard_map.64.k_ref.v_ref, bf16[2,4,2048,128]{3,2,1,0:T(8,128)(2,1)S(1)} %shard_map.64.k_ref.v_ref, ...), custom_call_target="tpu_custom_call" | custom-call | flops 603979776 | bytes 1048576 | tf_op jit(solution)/shard_map/pallas_call | solution.py:232
  15.1 2.3 %shard_map.69 = (bf16[1,272,128]{2,1,0:T(8,128)(2,1)S(1)}, f32[1,256,128]{2,1,0:T(8,128)S(1)}, f32[1,256,128]{2,1,0:T(8,128)S(1)}) custom-call(bf16[4,16,4,8,128]{4,3,2,1,0:T(8,128)(2,1)S(1)} %copy-done.1, bf16[2,4,2048,128]{3,2,1,0:T(8,128)(2,1)S(1)} %shard_map.64.k_ref.v_ref, bf16[2,4,2048,128]{3,2,1,0:T(8,128)(2,1)S(1)} %shard_map.64.k_ref.v_ref, ...), custom_call_target="tpu_custom_call" | custom-call | flops 603979776 | bytes 1048576 | tf_op jit(solution)/shard_map/pallas_call | solution.py:232
  17.4 1.9 %collective-permute-start.10 = (bf16[1,272,128]{2,1,0:T(8,128)(2,1)S(1)}, bf16[1,272,128]{2,1,0:T(8,128)(2,1)S(1)}, u32[]{:S(2)}, u32[]{:S(2)}) collective-permute-start(bf16[1,272,128]{2,1,0:T(8,128)(2,1)S(1)} %get-tuple-element.32), channel_id=1, source_target_pairs={{0,4},{4,0},{8,12},{12,8},{1,5},{5,1},{9,13},{13,9},{2,6},{6,2},{1... | collective-permute-start | bytes 208904 | tf_op jit(solution)/shard_map/ppermute | solution.py:369
  19.3 0.2 collective-permute-start.7
  19.5 1.8 %collective-permute-start.4 = (bf16[1,272,128]{2,1,0:T(8,128)(2,1)S(1)}, bf16[1,272,128]{2,1,0:T(8,128)(2,1)S(1)}, u32[]{:S(2)}, u32[]{:S(2)}) collective-permute-start(bf16[1,272,128]{2,1,0:T(8,128)(2,1)S(1)} %get-tuple-element.26), channel_id=1, source_target_pairs={{0,4},{4,0},{8,12},{12,8},{1,5},{5,1},{9,13},{13,9},{2,6},{6,2},{1... | collective-permute-start | bytes 208904 | tf_op jit(solution)/shard_map/ppermute | solution.py:369
  21.3 2.3 %shard_map.66 = (bf16[1,272,128]{2,1,0:T(8,128)(2,1)S(1)}, f32[1,256,128]{2,1,0:T(8,128)S(1)}, f32[1,256,128]{2,1,0:T(8,128)S(1)}) custom-call(bf16[4,16,4,8,128]{4,3,2,1,0:T(8,128)(2,1)S(1)} %copy-done.1, bf16[2,4,2048,128]{3,2,1,0:T(8,128)(2,1)S(1)} %shard_map.64.k_ref.v_ref, bf16[2,4,2048,128]{3,2,1,0:T(8,128)(2,1)S(1)} %shard_map.64.k_ref.v_ref, ...), custom_call_target="tpu_custom_call" | custom-call | flops 603979776 | bytes 1048576 | tf_op jit(solution)/shard_map/pallas_call | solution.py:232
  23.6 0.3 collective-permute-start.1
  23.9 0.0 collective-permute-done.10.got_ref
  23.9 0.3 shard_map.76.mine_ref
  24.2 2.9 %collective-permute-start.11 = (bf16[1,272,128]{2,1,0:T(8,128)(2,1)S(1)}, bf16[1,272,128]{2,1,0:T(8,128)(2,1)S(1)}, u32[]{:S(2)}, u32[]{:S(2)}) collective-permute-start(bf16[1,272,128]{2,1,0:T(8,128)(2,1)S(1)} %shard_map.76.mine_ref), channel_id=1, source_target_pairs={{0,8},{4,12},{8,0},{12,4},{1,9},{5,13},{9,1},{13,5},{2,10},{6,14},... | collective-permute-start | bytes 208904 | tf_op jit(solution)/shard_map/ppermute | solution.py:369
  27.1 0.0 collective-permute-done.7.got_ref
  27.1 0.3 shard_map.73.mine_ref
  27.4 0.2 collective-permute-start.8
  27.6 0.0 collective-permute-done.4.got_ref
  27.6 0.3 shard_map.70.mine_ref
  27.9 2.9 %collective-permute-start.5 = (bf16[1,272,128]{2,1,0:T(8,128)(2,1)S(1)}, bf16[1,272,128]{2,1,0:T(8,128)(2,1)S(1)}, u32[]{:S(2)}, u32[]{:S(2)}) collective-permute-start(bf16[1,272,128]{2,1,0:T(8,128)(2,1)S(1)} %shard_map.70.mine_ref), channel_id=1, source_target_pairs={{0,8},{4,12},{8,0},{12,4},{1,9},{5,13},{9,1},{13,5},{2,10},{6,14},... | collective-permute-start | bytes 208904 | tf_op jit(solution)/shard_map/ppermute | solution.py:369
  30.8 0.0 collective-permute-done.1.got_ref
  30.8 0.3 shard_map.67.mine_ref
  31.1 0.2 collective-permute-start.2
  31.4 1.1 %collective-permute-done.11.got_ref = bf16[1,272,128]{2,1,0:T(8,128)(2,1)S(1)} collective-permute-done((bf16[1,272,128]{2,1,0:T(8,128)(2,1)S(1)}, bf16[1,272,128]{2,1,0:T(8,128)(2,1)S(1)}, u32[]{:S(2)}, u32[]{:S(2)}) %collective-permute-start.11) | collective-permute-done | bytes 69664 | tf_op jit(solution)/shard_map/ppermute | solution.py:369
  32.4 0.3 shard_map.77.refs_6_
  32.8 2.2 %collective-permute-start.12 = (bf16[1,256,128]{2,1,0:T(8,128)(2,1)S(1)}, bf16[1,256,128]{2,1,0:T(8,128)(2,1)S(1)}, u32[]{:S(2)}, u32[]{:S(2)}) collective-permute-start(bf16[1,256,128]{2,1,0:T(8,128)(2,1)S(1)} %shard_map.77.refs_6_), channel_id=1, source_target_pairs={{0,4},{4,0},{8,12},{12,8},{1,5},{5,1},{9,13},{13,9},{2,6},{6,2},{1... | collective-permute-start | bytes 196616 | tf_op jit(solution)/shard_map/ppermute | solution.py:369
  35.0 1.2 %collective-permute-done.8.got_ref = bf16[1,272,128]{2,1,0:T(8,128)(2,1)S(1)} collective-permute-done((bf16[1,272,128]{2,1,0:T(8,128)(2,1)S(1)}, bf16[1,272,128]{2,1,0:T(8,128)(2,1)S(1)}, u32[]{:S(2)}, u32[]{:S(2)}) %collective-permute-start.8) | collective-permute-done | bytes 69664 | tf_op jit(solution)/shard_map/ppermute | solution.py:369
  36.2 0.3 shard_map.74.refs_4_
  36.5 1.0 %collective-permute-start.9 = (bf16[1,256,128]{2,1,0:T(8,128)(2,1)S(1)}, bf16[1,256,128]{2,1,0:T(8,128)(2,1)S(1)}, u32[]{:S(2)}, u32[]{:S(2)}) collective-permute-start(bf16[1,256,128]{2,1,0:T(8,128)(2,1)S(1)} %shard_map.74.refs_4_), channel_id=1, source_target_pairs={{0,4},{4,0},{8,12},{12,8},{1,5},{5,1},{9,13},{13,9},{2,6},{6,2},{1... | collective-permute-start | bytes 196616 | tf_op jit(solution)/shard_map/ppermute | solution.py:369
  37.5 0.8 %collective-permute-done.5.got_ref = bf16[1,272,128]{2,1,0:T(8,128)(2,1)S(1)} collective-permute-done((bf16[1,272,128]{2,1,0:T(8,128)(2,1)S(1)}, bf16[1,272,128]{2,1,0:T(8,128)(2,1)S(1)}, u32[]{:S(2)}, u32[]{:S(2)}) %collective-permute-start.5) | collective-permute-done | bytes 69664 | tf_op jit(solution)/shard_map/ppermute | solution.py:369
  38.3 0.3 shard_map.71.refs_2_
  38.6 0.4 collective-permute-start.6
  39.0 0.0 collective-permute-done.2.got_ref
  39.0 0.3 shard_map.68.refs_0_
  39.4 1.7 %collective-permute-start.3 = (bf16[1,256,128]{2,1,0:T(8,128)(2,1)S(1)}, bf16[1,256,128]{2,1,0:T(8,128)(2,1)S(1)}, u32[]{:S(2)}, u32[]{:S(2)}) collective-permute-start(bf16[1,256,128]{2,1,0:T(8,128)(2,1)S(1)} %shard_map.68.refs_0_), channel_id=1, source_target_pairs={{0,4},{4,0},{8,12},{12,8},{1,5},{5,1},{9,13},{13,9},{2,6},{6,2},{1... | collective-permute-start | bytes 196616 | tf_op jit(solution)/shard_map/ppermute | solution.py:369
  41.1 0.0 collective-permute-done.12.refs_7_
  41.1 0.0 collective-permute-done.9.refs_5_
  41.1 1.8 %collective-permute-done.6.refs_3_ = bf16[1,256,128]{2,1,0:T(8,128)(2,1)S(1)} collective-permute-done((bf16[1,256,128]{2,1,0:T(8,128)(2,1)S(1)}, bf16[1,256,128]{2,1,0:T(8,128)(2,1)S(1)}, u32[]{:S(2)}, u32[]{:S(2)}) %collective-permute-start.6) | collective-permute-done | bytes 65568 | tf_op jit(solution)/shard_map/ppermute | solution.py:369
  42.9 0.8 %collective-permute-done.3.refs_1_ = bf16[1,256,128]{2,1,0:T(8,128)(2,1)S(1)} collective-permute-done((bf16[1,256,128]{2,1,0:T(8,128)(2,1)S(1)}, bf16[1,256,128]{2,1,0:T(8,128)(2,1)S(1)}, u32[]{:S(2)}, u32[]{:S(2)}) %collective-permute-start.3) | collective-permute-done | bytes 65568 | tf_op jit(solution)/shard_map/ppermute | solution.py:369
  43.7 0.9 %shard_map.78 = bf16[4,16,4,8,128]{4,3,2,1,0:T(8,128)(2,1)} custom-call(bf16[1,256,128]{2,1,0:T(8,128)(2,1)S(1)} %shard_map.68.refs_0_, bf16[1,256,128]{2,1,0:T(8,128)(2,1)S(1)} %collective-permute-done.3.refs_1_, bf16[1,256,128]{2,1,0:T(8,128)(2,1)S(1)} %shard_map.71.refs_2_, bf16[1,256,128]{2,1,0:T(8,128)(2,1)S(1)} %collective-permute-done.6.refs_3_, ...), custom_call_target="tpu_custom_call" | custom-call | bytes 1048576 | tf_op jit(solution)/shard_map/pallas_call | solution.py:353
  (5 shorter events, 0.0 us)
Async XLA Ops:
  0.0 0.9 %copy-start = (bf16[4,2,16,4,128]{4,3,2,1,0:T(4,128)(2,1)S(1)}, bf16[4,2,16,4,128]{4,3,2,1,0:T(4,128)(2,1)}, u32[]{:S(2)}) copy-start(bf16[4,2,16,4,128]{4,3,2,1,0:T(4,128)(2,1)} %param.9) | copy-start | bytes 393220
  1.9 7.2 %collective-permute-start = (bf16[2,320,128]{2,1,0:T(8,128)(2,1)S(1)}, bf16[2,320,128]{2,1,0:T(8,128)(2,1)S(1)}, u32[]{:S(2)}, u32[]{:S(2)}) collective-permute-start(bf16[2,320,128]{2,1,0:T(8,128)(2,1)S(1)} %bitcast.6), channel_id=1, source_target_pairs={{0,2},{2,0},{1,3},{3,1},{4,6},{6,4},{5,7},{7,5},{8,10},{10,8},{9,1... | collective-permute-start | bytes 491528 | tf_op jit(solution)/shard_map/ppermute | solution.py:377
  5.0 2.2 %copy-start.2 = (bf16[2,2048,4,128]{3,2,1,0:T(4,128)(2,1)S(1)}, bf16[2,2048,4,128]{3,2,1,0:T(4,128)(2,1)}, u32[]{:S(2)}) copy-start(bf16[2,2048,4,128]{3,2,1,0:T(4,128)(2,1)} %param.7) | copy-start | bytes 12582916
  7.1 2.0 %copy-start.3 = (s32[4,32]{1,0:T(4,128)S(1)}, s32[4,32]{1,0:T(4,128)}, u32[]{:S(2)}) copy-start(s32[4,32]{1,0:T(4,128)} %refs_2_.1) | copy-start | bytes 1540
  7.1 2.0 %copy-start.4 = (s32[32]{0:T(128)S(1)}, s32[32]{0:T(128)}, u32[]{:S(2)}) copy-start(s32[32]{0:T(128)} %param.11) | copy-start | bytes 388
  7.1 3.4 %copy-start.1 = (bf16[4,16,4,8,128]{4,3,2,1,0:T(8,128)(2,1)S(1)}, bf16[4,16,4,8,128]{4,3,2,1,0:T(8,128)(2,1)}, u32[]{:S(2)}) copy-start(bf16[4,16,4,8,128]{4,3,2,1,0:T(8,128)(2,1)} %q_ref.7) | copy-start | bytes 1572868
  17.4 6.5 %collective-permute-start.10 = (bf16[1,272,128]{2,1,0:T(8,128)(2,1)S(1)}, bf16[1,272,128]{2,1,0:T(8,128)(2,1)S(1)}, u32[]{:S(2)}, u32[]{:S(2)}) collective-permute-start(bf16[1,272,128]{2,1,0:T(8,128)(2,1)S(1)} %get-tuple-element.32), channel_id=1, source_target_pairs={{0,4},{4,0},{8,12},{12,8},{1,5},{5,1},{9,13},{13,9},{2,6},{6,2},{1... | collective-permute-start | bytes 208904 | tf_op jit(solution)/shard_map/ppermute | solution.py:369
  19.3 7.8 %collective-permute-start.7 = (bf16[1,272,128]{2,1,0:T(8,128)(2,1)S(1)}, bf16[1,272,128]{2,1,0:T(8,128)(2,1)S(1)}, u32[]{:S(2)}, u32[]{:S(2)}) collective-permute-start(bf16[1,272,128]{2,1,0:T(8,128)(2,1)S(1)} %get-tuple-element.29), channel_id=1, source_target_pairs={{0,4},{4,0},{8,12},{12,8},{1,5},{5,1},{9,13},{13,9},{2,6},{6,2},{1... | collective-permute-start | bytes 208904 | tf_op jit(solution)/shard_map/ppermute | solution.py:369
  19.5 8.1 %collective-permute-start.4 = (bf16[1,272,128]{2,1,0:T(8,128)(2,1)S(1)}, bf16[1,272,128]{2,1,0:T(8,128)(2,1)S(1)}, u32[]{:S(2)}, u32[]{:S(2)}) collective-permute-start(bf16[1,272,128]{2,1,0:T(8,128)(2,1)S(1)} %get-tuple-element.26), channel_id=1, source_target_pairs={{0,4},{4,0},{8,12},{12,8},{1,5},{5,1},{9,13},{13,9},{2,6},{6,2},{1... | collective-permute-start | bytes 208904 | tf_op jit(solution)/shard_map/ppermute | solution.py:369
  23.6 7.2 %collective-permute-start.1 = (bf16[1,272,128]{2,1,0:T(8,128)(2,1)S(1)}, bf16[1,272,128]{2,1,0:T(8,128)(2,1)S(1)}, u32[]{:S(2)}, u32[]{:S(2)}) collective-permute-start(bf16[1,272,128]{2,1,0:T(8,128)(2,1)S(1)} %get-tuple-element.23), channel_id=1, source_target_pairs={{0,4},{4,0},{8,12},{12,8},{1,5},{5,1},{9,13},{13,9},{2,6},{6,2},{1... | collective-permute-start | bytes 208904 | tf_op jit(solution)/shard_map/ppermute | solution.py:369
  24.2 8.3 %collective-permute-start.11 = (bf16[1,272,128]{2,1,0:T(8,128)(2,1)S(1)}, bf16[1,272,128]{2,1,0:T(8,128)(2,1)S(1)}, u32[]{:S(2)}, u32[]{:S(2)}) collective-permute-start(bf16[1,272,128]{2,1,0:T(8,128)(2,1)S(1)} %shard_map.76.mine_ref), channel_id=1, source_target_pairs={{0,8},{4,12},{8,0},{12,4},{1,9},{5,13},{9,1},{13,5},{2,10},{6,14},... | collective-permute-start | bytes 208904 | tf_op jit(solution)/shard_map/ppermute | solution.py:369
  27.4 8.7 %collective-permute-start.8 = (bf16[1,272,128]{2,1,0:T(8,128)(2,1)S(1)}, bf16[1,272,128]{2,1,0:T(8,128)(2,1)S(1)}, u32[]{:S(2)}, u32[]{:S(2)}) collective-permute-start(bf16[1,272,128]{2,1,0:T(8,128)(2,1)S(1)} %shard_map.73.mine_ref), channel_id=1, source_target_pairs={{0,8},{4,12},{8,0},{12,4},{1,9},{5,13},{9,1},{13,5},{2,10},{6,14},... | collective-permute-start | bytes 208904 | tf_op jit(solution)/shard_map/ppermute | solution.py:369
  27.9 10.4 %collective-permute-start.5 = (bf16[1,272,128]{2,1,0:T(8,128)(2,1)S(1)}, bf16[1,272,128]{2,1,0:T(8,128)(2,1)S(1)}, u32[]{:S(2)}, u32[]{:S(2)}) collective-permute-start(bf16[1,272,128]{2,1,0:T(8,128)(2,1)S(1)} %shard_map.70.mine_ref), channel_id=1, source_target_pairs={{0,8},{4,12},{8,0},{12,4},{1,9},{5,13},{9,1},{13,5},{2,10},{6,14},... | collective-permute-start | bytes 208904 | tf_op jit(solution)/shard_map/ppermute | solution.py:369
  31.1 7.9 %collective-permute-start.2 = (bf16[1,272,128]{2,1,0:T(8,128)(2,1)S(1)}, bf16[1,272,128]{2,1,0:T(8,128)(2,1)S(1)}, u32[]{:S(2)}, u32[]{:S(2)}) collective-permute-start(bf16[1,272,128]{2,1,0:T(8,128)(2,1)S(1)} %shard_map.67.mine_ref), channel_id=1, source_target_pairs={{0,8},{4,12},{8,0},{12,4},{1,9},{5,13},{9,1},{13,5},{2,10},{6,14},... | collective-permute-start | bytes 208904 | tf_op jit(solution)/shard_map/ppermute | solution.py:369
  32.8 8.3 %collective-permute-start.12 = (bf16[1,256,128]{2,1,0:T(8,128)(2,1)S(1)}, bf16[1,256,128]{2,1,0:T(8,128)(2,1)S(1)}, u32[]{:S(2)}, u32[]{:S(2)}) collective-permute-start(bf16[1,256,128]{2,1,0:T(8,128)(2,1)S(1)} %shard_map.77.refs_6_), channel_id=1, source_target_pairs={{0,4},{4,0},{8,12},{12,8},{1,5},{5,1},{9,13},{13,9},{2,6},{6,2},{1... | collective-permute-start | bytes 196616 | tf_op jit(solution)/shard_map/ppermute | solution.py:369
  36.5 4.6 %collective-permute-start.9 = (bf16[1,256,128]{2,1,0:T(8,128)(2,1)S(1)}, bf16[1,256,128]{2,1,0:T(8,128)(2,1)S(1)}, u32[]{:S(2)}, u32[]{:S(2)}) collective-permute-start(bf16[1,256,128]{2,1,0:T(8,128)(2,1)S(1)} %shard_map.74.refs_4_), channel_id=1, source_target_pairs={{0,4},{4,0},{8,12},{12,8},{1,5},{5,1},{9,13},{13,9},{2,6},{6,2},{1... | collective-permute-start | bytes 196616 | tf_op jit(solution)/shard_map/ppermute | solution.py:369
  38.6 4.3 %collective-permute-start.6 = (bf16[1,256,128]{2,1,0:T(8,128)(2,1)S(1)}, bf16[1,256,128]{2,1,0:T(8,128)(2,1)S(1)}, u32[]{:S(2)}, u32[]{:S(2)}) collective-permute-start(bf16[1,256,128]{2,1,0:T(8,128)(2,1)S(1)} %shard_map.71.refs_2_), channel_id=1, source_target_pairs={{0,4},{4,0},{8,12},{12,8},{1,5},{5,1},{9,13},{13,9},{2,6},{6,2},{1... | collective-permute-start | bytes 196616 | tf_op jit(solution)/shard_map/ppermute | solution.py:369
  39.4 4.3 %collective-permute-start.3 = (bf16[1,256,128]{2,1,0:T(8,128)(2,1)S(1)}, bf16[1,256,128]{2,1,0:T(8,128)(2,1)S(1)}, u32[]{:S(2)}, u32[]{:S(2)}) collective-permute-start(bf16[1,256,128]{2,1,0:T(8,128)(2,1)S(1)} %shard_map.68.refs_0_), channel_id=1, source_target_pairs={{0,4},{4,0},{8,12},{12,8},{1,5},{5,1},{9,13},{13,9},{2,6},{6,2},{1... | collective-permute-start | bytes 196616 | tf_op jit(solution)/shard_map/ppermute | solution.py:369

commit v2 on v1

v2 whole, which is shorter than its diff:
```python
import functools
import math

import jax
import jax.numpy as jnp
from jax import lax
from jax.experimental import pallas as pl
from jax.experimental.pallas import tpu as pltpu
from jax.sharding import PartitionSpec as P

LANES = 128
HIDDEN = -1e30
NN = (((1,), (0,)), ((), ()))
NT = (((1,), (1,)), ((), ()))
SMALL = pl.CostEstimate(flops=0, bytes_accessed=4096, transcendentals=0)


def round_up(value, multiple):
    return -(-value // multiple) * multiple


def dot(a, b, dims):
    return lax.dot_general(a, b, dims, preferred_element_type=jnp.float32)


def eye_mask(rows):
    shape = (rows, LANES)
    return lax.broadcasted_iota(jnp.int32, shape, 0) == lax.broadcasted_iota(jnp.int32, shape, 1)


def column_to_lanes(column):
    rows = column.shape[0]
    block = min(rows, LANES)
    mask = eye_mask(block)
    return jnp.concatenate(
        [
            jnp.sum(jnp.where(mask, column[at : at + block], 0.0), axis=0, keepdims=True)
            for at in range(0, rows, block)
        ],
        axis=0,
    )


def lanes_to_column(lanes, rows):
    block = min(rows, LANES)
    mask = eye_mask(block)
    return jnp.concatenate(
        [
            jnp.sum(jnp.where(mask, lanes[i : i + 1], 0.0), axis=1, keepdims=True)
            for i in range(lanes.shape[0])
        ],
        axis=0,
    )


def tail_rows(rows):
    return round_up(3 * -(-rows // LANES), 16)


def pack_tail(column):
    lanes = column_to_lanes(column)
    high = lanes.astype(jnp.bfloat16).astype(jnp.float32)
    middle = (lanes - high).astype(jnp.bfloat16).astype(jnp.float32)
    low = lanes - high - middle
    parts = jnp.concatenate([high, middle, low], axis=0)
    spare = tail_rows(column.shape[0]) - parts.shape[0]
    return jnp.concatenate([parts, jnp.zeros((spare, LANES), jnp.float32)], axis=0).astype(
        jnp.bfloat16
    )


def unpack_tail(tail, rows):
    tail = tail.astype(jnp.float32)
    blocks = -(-rows // LANES)
    lanes = tail[:blocks] + tail[blocks : 2 * blocks] + tail[2 * blocks : 3 * blocks]
    return lanes_to_column(lanes, rows)


def in_hbm(array):
    return pltpu.with_memory_space_constraint(array, pltpu.HBM)


def message_kernel(heads, suffix_ref, new_ref, out_ref, here, wide, sems):
    rows, each = suffix_ref.shape[1], new_ref.shape[2]
    total = here.shape[1]
    count = (total - rows) // each
    first = jnp.minimum(lax.axis_index("ctx") * count, new_ref.shape[0] - count)
    copies = [pltpu.make_async_copy(suffix_ref, here.at[:, pl.ds(0, rows)], sems.at[0])]
    for token in range(count):
        there = here.at[:, pl.ds(rows + token * each, each)]
        copies.append(pltpu.make_async_copy(new_ref.at[first + token], there, sems.at[1 + token]))
    for copy in copies:
        copy.start()
    for copy in copies:
        copy.wait()
    for kind in range(2):
        wide[kind] = here[kind].astype(jnp.float32)
        for head in range(heads):
            part = wide[kind, pl.ds(head, total // heads, stride=heads), :]
            out_ref[kind, head] = part.astype(out_ref.dtype)


def build_message(suffix, new, heads, tokens_dev):
    rows = suffix.shape[1] + tokens_dev * new.shape[2]
    size = suffix.shape[2]
    return pl.pallas_call(
        functools.partial(message_kernel, heads),
        in_specs=[pl.BlockSpec(memory_space=pltpu.HBM)] * 2,
        out_shape=jax.ShapeDtypeStruct((2, heads, rows // heads, size), suffix.dtype),
        scratch_shapes=[
            pltpu.VMEM((2, rows, size), suffix.dtype),
            pltpu.VMEM((2, rows, size), jnp.float32),
            pltpu.SemaphoreType.DMA((1 + tokens_dev,)),
        ],
        compiler_params=pltpu.CompilerParams(vmem_limit_bytes=16 << 20),
        cost_estimate=SMALL,
    )(in_hbm(suffix), in_hbm(new))


def iota(shape, axis):
    return lax.broadcasted_iota(jnp.int32, shape, axis)


def lineage_bias(ancestors_ref, lengths_ref, owners, per_owner, suffix_dev, tokens_dev, padded):
    particles = owners * per_owner
    steps = ancestors_ref.shape[0]
    suffix_columns = per_owner * suffix_dev
    each = suffix_columns + per_owner * tokens_dev
    my_owner = lax.axis_index("dom")
    my_shard = lax.axis_index("ctx")
    square = (particles, particles)
    same = iota(square, 0) == iota(square, 1)

    def as_column(row):
        return jnp.sum(jnp.where(same, row, 0), axis=1, keepdims=True)

    unit = same.astype(jnp.float32)
    nothing = jnp.zeros((particles, tokens_dev * particles), jnp.float32)
    state = jnp.concatenate([unit, nothing], axis=1)
    pick = iota((per_owner, particles), 1) == iota((per_owner, particles), 0) + my_owner * per_owner
    pick = pick.astype(jnp.bfloat16)
    mine = []
    for step in range(steps):
        parent = as_column(ancestors_ref[step : step + 1, :])
        move = (parent == iota(square, 1)).astype(jnp.bfloat16)
        state = dot(move, state.astype(jnp.bfloat16), NN)
        blocks = [state[:, :particles]]
        for token in range(tokens_dev):
            written = my_shard * tokens_dev + token
            old = state[:, (1 + token) * particles : (2 + token) * particles]
            blocks.append(jnp.where(written == step, unit, old))
        state = jnp.concatenate(blocks, axis=1)
        mine.append(dot(pick, state.astype(jnp.bfloat16), NN))
    mine = jnp.concatenate(mine, axis=0).astype(jnp.bfloat16)
    lengths = as_column(lengths_ref[...])
    shape = (particles, padded)
    column = iota(shape, 1)
    source = column // each
    owner = lax.rem(my_owner + owners - source, owners)
    inner = column - source * each
    after = inner - suffix_columns
    in_suffix = after < 0
    local = jnp.where(in_suffix, inner // suffix_dev, lax.rem(jnp.maximum(after, 0), per_owner))
    here = (iota(shape, 0) == owner * per_owner + local) & (column < owners * each)
    position = my_shard * suffix_dev + lax.rem(inner, suffix_dev)
    seen = [here & in_suffix & (position < lengths)]
    for token in range(tokens_dev):
        seen.append(here & (after >= token * per_owner) & (after < (token + 1) * per_owner))
    table = jnp.concatenate([s.astype(jnp.bfloat16) for s in seen], axis=0)
    return jnp.where(dot(mine, table, NN) > 0.5, 0.0, HIDDEN)


def split_kernel(
    heads, block, owners, suffix_dev, tokens_dev,
    rows_ref, ancestors_ref, lengths_ref, out_ref, bias_ref, here, wide, sems,
):
    total = out_ref.shape[2]
    places = [(kind, at) for kind in range(2) for at in range(0, total, block)]
    copies = [
        pltpu.make_async_copy(
            rows_ref.at[kind, pl.ds(at * heads, block * heads)],
            here.at[kind, pl.ds(at * heads, block * heads)],
            sems.at[i],
        )
        for i, (kind, at) in enumerate(places)
    ]
    for copy in copies:
        copy.start()
    bias_ref[...] = lineage_bias(
        ancestors_ref,
        lengths_ref,
        owners,
        ancestors_ref.shape[1] // owners,
        suffix_dev,
        tokens_dev,
        bias_ref.shape[1],
    )
    for i, (kind, at) in enumerate(places):
        copies[i].wait()
        wide[i % 2] = here[kind, at * heads : (at + block) * heads].astype(jnp.float32)
        for head in range(heads):
            part = wide[i % 2, pl.ds(head, block, stride=heads), :]
            out_ref[kind, head, at : at + block] = part.astype(out_ref.dtype)


def split_prompt(rows, ancestors, lengths, heads, owners, suffix_dev, tokens_dev):
    total = rows.shape[1] // heads
    block = math.gcd(total, 512)
    size = rows.shape[2]
    steps, particles = ancestors.shape
    padded = round_up(particles * (suffix_dev + tokens_dev), LANES)
    return pl.pallas_call(
        functools.partial(split_kernel, heads, block, owners, suffix_dev, tokens_dev),
        in_specs=[pl.BlockSpec(memory_space=pltpu.HBM)]
        + [pl.BlockSpec(memory_space=pltpu.VMEM)] * 2,
        out_shape=(
            jax.ShapeDtypeStruct((2, heads, total, size), rows.dtype),
            jax.ShapeDtypeStruct((steps * particles // owners, padded), jnp.float32),
        ),
        scratch_shapes=[
            pltpu.VMEM(rows.shape, rows.dtype),
            pltpu.VMEM((2, block * heads, size), jnp.float32),
            pltpu.SemaphoreType.DMA((2 * total // block,)),
        ],
        compiler_params=pltpu.CompilerParams(vmem_limit_bytes=24 << 20),
        cost_estimate=SMALL,
    )(in_hbm(rows), ancestors, lengths.reshape(1, -1))


def with_ones(values):
    return jnp.concatenate([values, jnp.ones_like(values)], axis=1)


def row_peak(scores):
    return jnp.max(scores, axis=1, keepdims=True)


def weigh(scores, factor, offset):
    return jnp.exp2(scores * factor - offset).astype(jnp.bfloat16)


def prompt_sum(q, k_ref, v_ref, i, factor, peak):
    total = k_ref.shape[2]
    block = math.gcd(total, 512)
    together = None
    for at in range(0, total, block):
        scores = dot(q, k_ref[0, i, at : at + block], NT)
        if at == 0:
            top = row_peak(scores)
            offset = (top if peak is None else jnp.maximum(top, peak)) * factor
        part = dot(weigh(scores, factor, offset), with_ones(v_ref[0, i, at : at + block]), NN)
        together = part if together is None else together + part
    return together, offset


def prompt_kernel(factor, q_ref, k_ref, v_ref, together_ref, offset_ref):
    steps, per_owner, _, group, size = q_ref.shape
    q = q_ref[...].reshape(steps * per_owner * group, size)
    together, offset = prompt_sum(q, k_ref, v_ref, 0, factor, None)
    together_ref[...] = together
    offset_ref[...] = jnp.broadcast_to(offset, offset_ref.shape)


def block_specs(queries, prompt, head, count):
    steps, per_owner, _, group, size = queries.shape
    total = prompt.shape[2]
    at = head // count
    return [
        pl.BlockSpec((steps, per_owner, count, group, size), lambda i: (0, 0, at, 0, 0)),
        pl.BlockSpec((1, count, total, size), lambda i: (0, at, 0, 0)),
        pl.BlockSpec((1, count, total, size), lambda i: (1, at, 0, 0)),
    ]


def whole(array):
    return pl.BlockSpec(array.shape, lambda i: (0,) * array.ndim)


def start_head(queries, prompt, head, factor):
    steps, per_owner, _, group, size = queries.shape
    rows = steps * per_owner * group
    shapes = (
        jax.ShapeDtypeStruct((rows, 2 * size), jnp.float32),
        jax.ShapeDtypeStruct((rows, LANES), jnp.float32),
    )
    return pl.pallas_call(
        functools.partial(prompt_kernel, factor),
        grid=(1,),
        in_specs=block_specs(queries, prompt, head, 1),
        out_specs=[whole(s) for s in shapes],
        out_shape=shapes,
        compiler_params=pltpu.CompilerParams(vmem_limit_bytes=24 << 20),
        cost_estimate=SMALL,
    )(queries, prompt, prompt)


def attend_kernel(factor, owners, halves, started, *refs):
    q_ref, k_ref, v_ref, bias_ref = refs[:4]
    row_refs = refs[4 : 4 + owners]
    begun = refs[4 + owners : 4 + owners + 2 * started]
    _, send_ref, keep_ref, sums_ref, out, log_sums = refs[4 + owners + 2 * started :]
    steps, per_owner, count, group, size = q_ref.shape
    padded = bias_ref.shape[1]
    rows = steps * per_owner * group
    half = rows // halves

    def queries_of(i, first, number):
        here = number * per_owner * group
        q = q_ref[pl.ds(first, number), :, i].reshape(here, size)
        at = pl.multiple_of(first * per_owner, per_owner)
        bias = bias_ref[pl.ds(at, number * per_owner), :]
        bias = jnp.broadcast_to(bias[:, None, :], (number * per_owner, group, padded))
        return q, dot(q, suffix_of(i, 0), NT) + bias.reshape(here, padded)

    def suffix_of(i, kind):
        pieces = [ref[kind, i] for ref in row_refs]
        columns = sum(piece.shape[0] for piece in pieces)
        if padded > columns:
            pieces.append(jnp.zeros((padded - columns, size), jnp.bfloat16))
        return jnp.concatenate(pieces, axis=0)

    def store(at, together, offset):
        sums = together[:, size:]
        out[pl.ds(at, sums.shape[0]), :] = together[:, :size] / sums
        log_sums[pl.ds(at, sums.shape[0]), :] = offset + jnp.log2(sums)
        return sums

    for i in range(count):
        q, suffix_scores = queries_of(i, 0, steps)
        if i < started:
            together, offset = begun[2 * i][...], begun[2 * i + 1][:, :1]
        else:
            peak = row_peak(suffix_scores)
            together, offset = prompt_sum(q, k_ref, v_ref, i, factor, peak)
        weight = weigh(suffix_scores, factor, offset)
        together = together + dot(weight, with_ones(suffix_of(i, 1)), NN)
        sums = store(0, together, offset)

        @pl.when(jnp.logical_not(jnp.max(sums) < 2.0**100))
        def _():
            @pl.loop(0, steps)
            def _(step):
                q, suffix_scores = queries_of(i, step, 1)
                scores = dot(q, k_ref[0, i], NT)
                offset = jnp.maximum(row_peak(scores), row_peak(suffix_scores)) * factor
                together = dot(weigh(scores, factor, offset), with_ones(v_ref[0, i]), NN)
                weight = weigh(suffix_scores, factor, offset)
                together = together + dot(weight, with_ones(suffix_of(i, 1)), NN)
                store(pl.multiple_of(step * per_owner * group, per_owner * group), together, offset)

        bit = lax.rem(lax.axis_index("ctx"), 2) if halves == 2 else 0
        there = pl.ds(pl.multiple_of((halves - 1 - bit) * half, half), half)
        send_ref[i, :half] = out[there, :].astype(jnp.bfloat16)
        send_ref[i, half:] = pack_tail(log_sums[there, :][:, :1])
        here = pl.ds(pl.multiple_of(bit * half, half), half)
        keep_ref[i] = out[here, :]
        sums_ref[i] = log_sums[here, :]


def attend(queries, prompt, bias, row_list, head, count, factor, halves, begun, after):
    steps, per_owner, heads, group, size = queries.shape
    rows = steps * per_owner * group
    half = rows // halves
    shapes = (
        jax.ShapeDtypeStruct((count, half + tail_rows(half), size), jnp.bfloat16),
        jax.ShapeDtypeStruct((count, half, size), jnp.float32),
        jax.ShapeDtypeStruct((count, half, LANES), jnp.float32),
    )
    slots = row_list[0].shape[2]
    row_spec = pl.BlockSpec((2, count, slots, size), lambda i: (0, head // count, 0, 0))
    return pl.pallas_call(
        functools.partial(attend_kernel, factor, len(row_list), halves, len(begun) // 2),
        grid=(1,),
        in_specs=[
            *block_specs(queries, prompt, head, count),
            whole(bias),
            *[row_spec] * len(row_list),
            *[whole(b) for b in begun],
            pl.BlockSpec(memory_space=pl.ANY),
        ],
        out_specs=[whole(s) for s in shapes],
        out_shape=shapes,
        scratch_shapes=[
            pltpu.VMEM((rows, size), jnp.float32),
            pltpu.VMEM((rows, LANES), jnp.float32),
        ],
        compiler_params=pltpu.CompilerParams(vmem_limit_bytes=32 << 20),
        cost_estimate=SMALL,
    )(queries, prompt, prompt, bias, *row_list, *begun, after)


def merge(out_a, sum_a, out_b, sum_b):
    top = jnp.maximum(sum_a, sum_b)
    weight_a = jnp.exp2(sum_a - top)
    weight_b = jnp.exp2(sum_b - top)
    total = weight_a + weight_b
    return (out_a * weight_a + out_b * weight_b) / total, top + jnp.log2(total)


def in_vmem(count):
    return [pl.BlockSpec(memory_space=pltpu.VMEM)] * count + [pl.BlockSpec(memory_space=pl.ANY)]


def merge_kernel(level, last, keep_ref, sums_ref, got_ref, _, *outs):
    rows = keep_ref.shape[1]
    for i in range(keep_ref.shape[0]):
        got_sum = unpack_tail(got_ref[i, rows:], rows)
        out, log_sum = merge(
            keep_ref[i], sums_ref[i][:, :1], got_ref[i, :rows].astype(jnp.float32), got_sum
        )
        if last:
            outs[0][i, :rows] = out.astype(jnp.bfloat16)
            outs[0][i, rows:] = pack_tail(log_sum)
        else:
            half = rows // 2
            bit = lax.rem(lax.axis_index("ctx") >> level, 2) == 1
            send, keep, wide = outs

            def choose(first, value):
                return jnp.where(first, value[:half], value[half:])

            send[i, :half] = choose(bit, out).astype(jnp.bfloat16)
            send[i, half:] = pack_tail(choose(bit, log_sum))
            keep[i] = choose(~bit, out)
            wide[i] = jnp.broadcast_to(choose(~bit, log_sum), (half, LANES))


def merge_parts(keep, sums, got, level, last, after):
    count, rows, size = keep.shape
    part = rows if last else rows // 2
    shapes = [jax.ShapeDtypeStruct((count, part + tail_rows(part), size), jnp.bfloat16)]
    if not last:
        shapes.append(jax.ShapeDtypeStruct((count, part, size), jnp.float32))
        shapes.append(jax.ShapeDtypeStruct((count, part, LANES), jnp.float32))
    return pl.pallas_call(
        functools.partial(merge_kernel, level, last),
        in_specs=in_vmem(3),
        out_shape=tuple(shapes),
        compiler_params=pltpu.CompilerParams(vmem_limit_bytes=16 << 20),
        cost_estimate=SMALL,
    )(keep, sums, got, after)


def finish_kernel(mine_ref, got_ref, _, out_ref):
    rows = math.prod(out_ref.shape[1:-1])
    for i in range(mine_ref.shape[0]):
        out, _ = merge(
            mine_ref[i, :rows].astype(jnp.float32),
            unpack_tail(mine_ref[i, rows:], rows),
            got_ref[i, :rows].astype(jnp.float32),
            unpack_tail(got_ref[i, rows:], rows),
        )
        out_ref[i] = out.astype(jnp.bfloat16).reshape(out_ref.shape[1:])


def finish(mine, got, shape, after):
    return pl.pallas_call(
        finish_kernel,
        in_specs=in_vmem(2),
        out_shape=jax.ShapeDtypeStruct(shape, jnp.bfloat16),
        compiler_params=pltpu.CompilerParams(vmem_limit_bytes=16 << 20),
        cost_estimate=SMALL,
    )(mine, got, after)


def place_kernel(levels, plan, *refs):
    *part_refs, out_ref, sems = refs
    copies = []
    for (head, own), ref in zip(plan, part_refs):
        blocks = ref.shape[1]
        bit = lax.rem(lax.axis_index("ctx"), 2) if levels > 1 else 0
        at = (bit if own else 1 - bit) * blocks
        for i in range(ref.shape[0]):
            there = out_ref.at[pl.ds(at, blocks), :, head + i]
            copies.append(pltpu.make_async_copy(ref.at[i], there, sems.at[len(copies)]))
    for copy in copies:
        copy.start()
    for copy in copies:
        copy.wait()


def place(parts, shape, levels):
    arrays = [array for array, _, _ in parts]
    plan = [(head, own) for _, head, own in parts]
    return pl.pallas_call(
        functools.partial(place_kernel, levels, plan),
        in_specs=[pl.BlockSpec(memory_space=pltpu.VMEM)] * len(arrays),
        out_specs=pl.BlockSpec(memory_space=pltpu.HBM),
        out_shape=jax.ShapeDtypeStruct(shape, jnp.bfloat16),
        scratch_shapes=[pltpu.SemaphoreType.DMA((sum(a.shape[0] for a in arrays),))],
        compiler_params=pltpu.CompilerParams(vmem_limit_bytes=16 << 20),
        cost_estimate=SMALL,
    )(*arrays)


def on_device(shards, owners, queries, prompt_cache, suffix_cache, new_kv, ancestors, lengths):
    steps, per_owner, heads, group, size = queries.shape
    suffix_dev = suffix_cache.shape[2]
    shard = lax.axis_index("ctx")
    factor = math.log2(math.e) / math.sqrt(size)
    tokens_dev = -(-steps // shards)
    levels = shards.bit_length() - 1
    halves = 2 if levels > 1 else 1

    def swap(value, bit):
        return lax.ppermute(value, "ctx", [(i, i ^ (1 << bit)) for i in range(shards)])

    mine = build_message(
        suffix_cache.reshape(2, -1, size), new_kv.reshape(steps, 2, -1, size), heads, tokens_dev
    )
    row_list = [mine] + [
        lax.ppermute(mine, "dom", [(i, (i + hop) % owners) for i in range(owners)])
        for hop in range(1, owners)
    ]
    prompt, bias = split_prompt(
        prompt_cache.reshape(2, -1, size), ancestors, lengths, heads, owners, suffix_dev, tokens_dev
    )
    last = [bias]

    def follow(results):
        last[0] = results[0] if isinstance(results, (tuple, list)) else results
        return results

    begun = follow(start_head(queries, prompt, 0, factor))
    first = max(heads // 2, 1)
    chunks = [(0, first)] + [(head, 1) for head in range(first, heads)]
    messages, kept, parts = {}, {}, []

    def run_attend(chunk):
        head, count = chunk
        send, keep, sums = follow(
            attend(
                queries, prompt, bias, row_list, head, count, factor, halves,
                begun if head == 0 else (), last[0],
            )
        )
        kept[chunk] = keep, sums
        messages[chunk] = send, swap(send, 0)

    def run_merges(chunk):
        for level in range(1, levels):
            results = follow(
                merge_parts(
                    *kept[chunk], messages[chunk][1], level, level == levels - 1, last[0]
                )
            )
            send, kept[chunk] = results[0], results[1:]
            messages[chunk] = send, swap(send, level)

    def run_finish(chunk):
        head, count = chunk
        blocks = (steps * per_owner) >> (levels - 1 if levels > 1 else 0)
        done = follow(finish(*messages[chunk], (count, blocks, group, size), last[0]))
        for level in range(levels - 2, 0, -1):
            other = swap(done, level)
            done = jnp.where(
                (shard >> level) % 2 == 1,
                jnp.concatenate([other, done], axis=1),
                jnp.concatenate([done, other], axis=1),
            )
        done = done.reshape(count, steps // halves, per_owner, group, size)
        parts.append((done, head, True))
        if levels > 1:
            parts.append((swap(done, 0), head, False))

    run_attend(chunks[0])
    for before, chunk in zip(chunks, chunks[1:]):
        run_attend(chunk)
        run_merges(before)
    run_merges(chunks[-1])
    for chunk in chunks[:-1]:
        run_finish(chunk)
    run_finish(chunks[-1])
    return place(parts, queries.shape, levels)


def solution(mesh):
    return jax.shard_map(
        functools.partial(on_device, mesh.shape["ctx"], mesh.shape["dom"]),
        mesh=mesh,
        in_specs=(
            P("groups", "dom", "tp", None, None),
            P("groups", "ctx", "tp", None),
            P("groups", "dom", "ctx", "tp", None),
            P("groups", None, "dom", "tp", None),
            P("groups", None),
            P("groups"),
        ),
        out_specs=P("groups", "dom", "tp", None, None),
        check_vma=False,
    )
```

time: 44.8 us -> 47.2 us (1.054); the launches traced: 44.6 us -> 47.5 us
  Pallas kernels: 15.5 us -> 22.9 us
  starting transfers between devices: 18.7 us -> 16.3 us
  local copies, waits for them, and re-layouts: 3.12 us -> 1.34 us
  other arithmetic: 1.02 us -> 0 us
  waiting for transfers between devices: 6.13 us -> 6.88 us
    pallas_call x15 -> x13, Pallas kernels: 15.5 us -> 22.9 us  [the longest x3 13.9 us: attend(): pl.pallas_call(functools.partial(attend_kernel, factor, len(row_list), ha...]
    ppermute x12 -> x9, starting transfers between devices: 15.7 us -> 13.3 us  [swap(): lax.ppermute(value, 'ctx', [(i, i ^ 1 << bit) for i in range(shards)])]
    unnamed x10 -> x6, local copies, waits for them, and re-layouts: 3.1 us -> 1.34 us
    ppermute x12 -> x9, waiting for transfers between devices: 5.61 us -> 6.87 us  [swap(): lax.ppermute(value, 'ctx', [(i, i ^ 1 << bit) for i in range(shards)])]
    concatenate x1 -> x0, other arithmetic: 1.02 us -> none  [on_device(): rows = jnp.concatenate([suffix_cache, jnp.moveaxis(tokens, 0, 2)], axis=2)]
    ppermute x1, waiting for transfers between devices: 0.53 us -> 0.01 us  [on_device(): lax.ppermute(mine, 'dom', [(i, (i + hop) % owners) for i in range(owners)])]
  transfers between devices with their start and end apart: 13 -> 10, of which waited for: 6 -> 5; matrix products, arithmetic and copies ran while one was open for 0% -> 0% of each run, Pallas kernels for 14% -> 30%
where the time goes in v2:
time: 47.2 us; the launch traced here: 47.5 us
  Pallas kernels  22.9 us (49%)
  starting transfers between devices  16.3 us (35%)
  waiting for transfers between devices  6.88 us (15%)
  local copies, waits for them, and re-layouts  1.34 us (3%)
    pallas_call x3, Pallas kernels, attend(): pl.pallas_call(functools.partial(attend_kernel, factor, len(row_list), ha...  13.9 us
    ppermute x9, starting transfers between devices, swap(): lax.ppermute(value, 'ctx', [(i, i ^ 1 << bit) for i in range(shards)])  13.3 us
    ppermute x9, waiting for transfers between devices, swap(): lax.ppermute(value, 'ctx', [(i, i ^ 1 << bit) for i in range(shards)])  6.87 us
    pallas_call x1, Pallas kernels, split_prompt(): pl.pallas_call(functools.partial(split_kernel, heads, block, owners, suff...  3.12 us
    ppermute x1, starting transfers between devices, on_device(): lax.ppermute(mine, 'dom', [(i, (i + hop) % owners) for i in range(owners)])  3 us
    pallas_call x1, Pallas kernels, start_head(): pl.pallas_call(functools.partial(prompt_kernel, factor), grid=(1,), in_sp...  1.66 us
    unnamed x6, local copies, waits for them, and re-layouts  1.34 us
    pallas_call x3, Pallas kernels, merge_parts(): pl.pallas_call(functools.partial(merge_kernel, level, last), in_specs=in_...  1.13 us
  transfers between devices with their start and end apart: 10, of which 5 were waited for; matrix products, arithmetic and copies ran while one was open for 0% of the time, Pallas kernels for 30%

profile of v2, /device:TPU:0, one launch (start us, length us, event | category | flops | bytes accessed | tf_op | source)
XLA Modules:
  0.0 47.5 jit_solution(3293475179788529483)
XLA Ops:
  0.0 0.0 copy-start
  0.0 1.0 %shard_map.65.refs_4_ = bf16[2,4,80,128]{3,2,1,0:T(8,128)(2,1)S(1)} custom-call(bf16[2,256,128]{2,1,0:T(8,128)(2,1)} %bitcast.15, bf16[4,2,64,128]{3,2,1,0:T(8,128)(2,1)} %bitcast.16), custom_call_target="tpu_custom_call" | custom-call | bytes 4096 | tf_op jit(solution)/shard_map/pallas_call | solution.py:106
  1.0 3.0 %collective-permute-start = (bf16[2,4,80,128]{3,2,1,0:T(8,128)(2,1)S(1)}, bf16[2,4,80,128]{3,2,1,0:T(8,128)(2,1)S(1)}, u32[]{:S(2)}, u32[]{:S(2)}) collective-permute-start(bf16[2,4,80,128]{3,2,1,0:T(8,128)(2,1)S(1)} %shard_map.65.refs_4_), channel_id=1, source_target_pairs={{0,2},{2,0},{1,3},{3,1},{4,6},{6,4},{5,7},{7,5},{8,10},{10,8},{9,1... | collective-permute-start | bytes 491528 | tf_op jit(solution)/shard_map/ppermute | solution.py:512
  4.0 0.0 copy-start.1
  4.0 0.7 %copy-done.1 = s32[4,32]{1,0:T(4,128)S(1)} copy-done((s32[4,32]{1,0:T(4,128)S(1)}, s32[4,32]{1,0:T(4,128)}, u32[]{:S(2)}) %copy-start.1) | copy-done | bytes 536
  4.7 0.0 copy-start.2
  4.7 0.7 %copy-done.2 = s32[32]{0:T(128)S(1)} copy-done((s32[32]{0:T(128)S(1)}, s32[32]{0:T(128)}, u32[]{:S(2)}) %copy-start.2) | copy-done | bytes 152
  5.4 3.1 %shard_map.64 = (bf16[2,4,2048,128]{3,2,1,0:T(8,128)(2,1)S(1)}, f32[64,256]{1,0:T(8,128)S(1)}) custom-call(bf16[2,8192,128]{2,1,0:T(8,128)(2,1)} %bitcast.14, s32[4,32]{1,0:T(4,128)S(1)} %copy-done.1, s32[1,32]{1,0:T(1,128)S(1)} %bitcast.13), custom_call_target="tpu_custom_call" | custom-call | bytes 4096 | tf_op jit(solution)/shard_map/pallas_call | solution.py:212
  8.5 0.0 copy-done
  8.5 1.7 %shard_map.66 = (f32[512,256]{1,0:T(8,128)S(1)}, f32[512,128]{1,0:T(8,128)S(1)}) custom-call(bf16[4,16,4,8,128]{4,3,2,1,0:T(8,128)(2,1)S(1)} %copy-done, bf16[2,4,2048,128]{3,2,1,0:T(8,128)(2,1)S(1)} %get-tuple-element.18.k_ref.v_ref.refs_1_.refs_2_, bf16[2,4,2048,128]{3,2,1,0:T(8,128)(2,1)S(1)} %get-tuple-element.18.k_ref.v_ref.refs_1_.refs_2_), custom_call_target="tpu_custom_call" | custom-call | bytes 4096 | tf_op jit(solution)/shard_map/pallas_call | solution.py:286
  10.2 0.0 collective-permute-done.refs_5_
  10.2 6.2 %shard_map.67 = (bf16[2,272,128]{2,1,0:T(8,128)(2,1)S(1)}, f32[2,256,128]{2,1,0:T(8,128)S(1)}, f32[2,256,128]{2,1,0:T(8,128)S(1)}) custom-call(bf16[4,16,4,8,128]{4,3,2,1,0:T(8,128)(2,1)S(1)} %copy-done, bf16[2,4,2048,128]{3,2,1,0:T(8,128)(2,1)S(1)} %get-tuple-element.18.k_ref.v_ref.refs_1_.refs_2_, ...), custom_call_target="tpu_custom_call" | custom-call | bytes 4096 | tf_op jit(solution)/shard_map/pallas_call | solution.py:371
  16.4 1.7 %collective-permute-start.1 = (bf16[2,272,128]{2,1,0:T(8,128)(2,1)S(1)}, bf16[2,272,128]{2,1,0:T(8,128)(2,1)S(1)}, u32[]{:S(2)}, u32[]{:S(2)}) collective-permute-start(bf16[2,272,128]{2,1,0:T(8,128)(2,1)S(1)} %get-tuple-element.24.refs_6_), channel_id=1, source_target_pairs={{0,4},{4,0},{8,12},{12,8},{1,5},{5,1},{9,13},{13,9},{2,6},{6,2},{1... | collective-permute-start | bytes 417800 | tf_op jit(solution)/shard_map/ppermute | solution.py:506
  18.1 5.7 %shard_map.68 = (bf16[1,272,128]{2,1,0:T(8,128)(2,1)S(1)}, f32[1,256,128]{2,1,0:T(8,128)S(1)}, f32[1,256,128]{2,1,0:T(8,128)S(1)}) custom-call(bf16[4,16,4,8,128]{4,3,2,1,0:T(8,128)(2,1)S(1)} %copy-done, bf16[2,4,2048,128]{3,2,1,0:T(8,128)(2,1)S(1)} %get-tuple-element.18.k_ref.v_ref.refs_1_.refs_2_, ...), custom_call_target="tpu_custom_call" | custom-call | bytes 4096 | tf_op jit(solution)/shard_map/pallas_call | solution.py:371
  23.8 0.0 collective-permute-done.1.got_ref
  23.8 0.5 shard_map.69.refs_6_.mine_ref
  24.2 0.4 collective-permute-start.2
  24.7 1.3 %collective-permute-start.4 = (bf16[1,272,128]{2,1,0:T(8,128)(2,1)S(1)}, bf16[1,272,128]{2,1,0:T(8,128)(2,1)S(1)}, u32[]{:S(2)}, u32[]{:S(2)}) collective-permute-start(bf16[1,272,128]{2,1,0:T(8,128)(2,1)S(1)} %get-tuple-element.25._), channel_id=1, source_target_pairs={{0,4},{4,0},{8,12},{12,8},{1,5},{5,1},{9,13},{13,9},{2,6},{6,2},{1... | collective-permute-start | bytes 208904 | tf_op jit(solution)/shard_map/ppermute | solution.py:506
  26.0 2.1 %shard_map.70 = (bf16[1,272,128]{2,1,0:T(8,128)(2,1)S(1)}, f32[1,256,128]{2,1,0:T(8,128)S(1)}, f32[1,256,128]{2,1,0:T(8,128)S(1)}) custom-call(bf16[4,16,4,8,128]{4,3,2,1,0:T(8,128)(2,1)S(1)} %copy-done, bf16[2,4,2048,128]{3,2,1,0:T(8,128)(2,1)S(1)} %get-tuple-element.18.k_ref.v_ref.refs_1_.refs_2_, ...), custom_call_target="tpu_custom_call" | custom-call | bytes 4096 | tf_op jit(solution)/shard_map/pallas_call | solution.py:371
  28.1 0.7 %collective-permute-start.3 = (bf16[1,272,128]{2,1,0:T(8,128)(2,1)S(1)}, bf16[1,272,128]{2,1,0:T(8,128)(2,1)S(1)}, u32[]{:S(2)}, u32[]{:S(2)}) collective-permute-start(bf16[1,272,128]{2,1,0:T(8,128)(2,1)S(1)} %get-tuple-element.28._), channel_id=1, source_target_pairs={{0,4},{4,0},{8,12},{12,8},{1,5},{5,1},{9,13},{13,9},{2,6},{6,2},{1... | collective-permute-start | bytes 208904 | tf_op jit(solution)/shard_map/ppermute | solution.py:506
  28.8 1.0 %collective-permute-done.4.got_ref = bf16[1,272,128]{2,1,0:T(8,128)(2,1)S(1)} collective-permute-done((bf16[1,272,128]{2,1,0:T(8,128)(2,1)S(1)}, bf16[1,272,128]{2,1,0:T(8,128)(2,1)S(1)}, u32[]{:S(2)}, u32[]{:S(2)}) %collective-permute-start.4) | collective-permute-done | bytes 69664 | tf_op jit(solution)/shard_map/ppermute | solution.py:506
  29.8 0.3 shard_map.71._.mine_ref
  30.2 3.2 %collective-permute-start.6 = (bf16[1,272,128]{2,1,0:T(8,128)(2,1)S(1)}, bf16[1,272,128]{2,1,0:T(8,128)(2,1)S(1)}, u32[]{:S(2)}, u32[]{:S(2)}) collective-permute-start(bf16[1,272,128]{2,1,0:T(8,128)(2,1)S(1)} %shard_map.71._.mine_ref), channel_id=1, source_target_pairs={{0,8},{4,12},{8,0},{12,4},{1,9},{5,13},{9,1},{13,5},{2,10},{6,14},... | collective-permute-start | bytes 208904 | tf_op jit(solution)/shard_map/ppermute | solution.py:506
  33.4 0.3 collective-permute-done.3.got_ref
  33.7 0.3 shard_map.72._.mine_ref
  34.0 3.7 %collective-permute-start.8 = (bf16[1,272,128]{2,1,0:T(8,128)(2,1)S(1)}, bf16[1,272,128]{2,1,0:T(8,128)(2,1)S(1)}, u32[]{:S(2)}, u32[]{:S(2)}) collective-permute-start(bf16[1,272,128]{2,1,0:T(8,128)(2,1)S(1)} %shard_map.72._.mine_ref), channel_id=1, source_target_pairs={{0,8},{4,12},{8,0},{12,4},{1,9},{5,13},{9,1},{13,5},{2,10},{6,14},... | collective-permute-start | bytes 208904 | tf_op jit(solution)/shard_map/ppermute | solution.py:506
  37.7 0.0 collective-permute-done.2.got_ref
  37.7 0.5 shard_map.73._
  38.2 0.1 collective-permute-start.5
  38.2 0.0 collective-permute-done.6.got_ref
  38.2 0.3 shard_map.74._
  38.6 2.1 %collective-permute-start.7 = (bf16[1,2,16,8,128]{4,3,2,1,0:T(8,128)(2,1)S(1)}, bf16[1,2,16,8,128]{4,3,2,1,0:T(8,128)(2,1)S(1)}, u32[]{:S(2)}, u32[]{:S(2)}) collective-permute-start(bf16[1,2,16,8,128]{4,3,2,1,0:T(8,128)(2,1)S(1)} %bitcast.9), channel_id=1, source_target_pairs={{0,4},{4,0},{8,12},{12,8},{1,5},{5,1},{9,13},{13,9},{2,6},{6,2},{1... | collective-permute-start | bytes 196616 | tf_op jit(solution)/shard_map/ppermute | solution.py:506
  40.6 1.3 %collective-permute-done.8.got_ref = bf16[1,272,128]{2,1,0:T(8,128)(2,1)S(1)} collective-permute-done((bf16[1,272,128]{2,1,0:T(8,128)(2,1)S(1)}, bf16[1,272,128]{2,1,0:T(8,128)(2,1)S(1)}, u32[]{:S(2)}, u32[]{:S(2)}) %collective-permute-start.8) | collective-permute-done | bytes 69664 | tf_op jit(solution)/shard_map/ppermute | solution.py:506
  42.0 0.3 shard_map.75
  42.3 0.1 collective-permute-start.9
  42.4 2.4 %collective-permute-done.7.refs_3_ = bf16[1,2,16,8,128]{4,3,2,1,0:T(8,128)(2,1)S(1)} collective-permute-done((bf16[1,2,16,8,128]{4,3,2,1,0:T(8,128)(2,1)S(1)}, bf16[1,2,16,8,128]{4,3,2,1,0:T(8,128)(2,1)S(1)}, u32[]{:S(2)}, u32[]{:S(2)}) %collective-permute-start.7) | collective-permute-done | bytes 65568 | tf_op jit(solution)/shard_map/ppermute | solution.py:506
  44.8 1.9 %collective-permute-done.9.refs_5_ = bf16[1,2,16,8,128]{4,3,2,1,0:T(8,128)(2,1)S(1)} collective-permute-done((bf16[1,2,16,8,128]{4,3,2,1,0:T(8,128)(2,1)S(1)}, bf16[1,2,16,8,128]{4,3,2,1,0:T(8,128)(2,1)S(1)}, u32[]{:S(2)}, u32[]{:S(2)}) %collective-permute-start.9) | collective-permute-done | bytes 65568 | tf_op jit(solution)/shard_map/ppermute | solution.py:506
  46.7 0.0 collective-permute-done.5.refs_1_
  46.7 0.8 %shard_map.76 = bf16[4,16,4,8,128]{4,3,2,1,0:T(8,128)(2,1)} custom-call(bf16[2,2,16,8,128]{4,3,2,1,0:T(8,128)(2,1)S(1)} %bitcast.8, bf16[2,2,16,8,128]{4,3,2,1,0:T(8,128)(2,1)S(1)} %collective-permute-done.5.refs_1_, bf16[1,2,16,8,128]{4,3,2,1,0:T(8,128)(2,1)S(1)} %bitcast.10, bf16[1,2,16,8,128]{4,3,2,1,0:T(8,128)(2,1)S(1)} %collective-permute-done.7.refs_3_, ...), custom_call_target="tpu_custom_call" | custom-call | bytes 4096 | tf_op jit(solution)/shard_map/pallas_call | solution.py:485
Async XLA Ops:
  0.0 8.5 %copy-start = (bf16[4,16,4,8,128]{4,3,2,1,0:T(8,128)(2,1)S(1)}, bf16[4,16,4,8,128]{4,3,2,1,0:T(8,128)(2,1)}, u32[]{:S(2)}) copy-start(bf16[4,16,4,8,128]{4,3,2,1,0:T(8,128)(2,1)} %refs_0_.5) | copy-start | bytes 1572868
  1.0 9.1 %collective-permute-start = (bf16[2,4,80,128]{3,2,1,0:T(8,128)(2,1)S(1)}, bf16[2,4,80,128]{3,2,1,0:T(8,128)(2,1)S(1)}, u32[]{:S(2)}, u32[]{:S(2)}) collective-permute-start(bf16[2,4,80,128]{3,2,1,0:T(8,128)(2,1)S(1)} %shard_map.65.refs_4_), channel_id=1, source_target_pairs={{0,2},{2,0},{1,3},{3,1},{4,6},{6,4},{5,7},{7,5},{8,10},{10,8},{9,1... | collective-permute-start | bytes 491528 | tf_op jit(solution)/shard_map/ppermute | solution.py:512
  4.0 0.7 %copy-start.1 = (s32[4,32]{1,0:T(4,128)S(1)}, s32[4,32]{1,0:T(4,128)}, u32[]{:S(2)}) copy-start(s32[4,32]{1,0:T(4,128)} %ancestors_ref.1) | copy-start | bytes 1540
  4.7 0.7 %copy-start.2 = (s32[32]{0:T(128)S(1)}, s32[32]{0:T(128)}, u32[]{:S(2)}) copy-start(s32[32]{0:T(128)} %param.11) | copy-start | bytes 388
  16.4 7.3 %collective-permute-start.1 = (bf16[2,272,128]{2,1,0:T(8,128)(2,1)S(1)}, bf16[2,272,128]{2,1,0:T(8,128)(2,1)S(1)}, u32[]{:S(2)}, u32[]{:S(2)}) collective-permute-start(bf16[2,272,128]{2,1,0:T(8,128)(2,1)S(1)} %get-tuple-element.24.refs_6_), channel_id=1, source_target_pairs={{0,4},{4,0},{8,12},{12,8},{1,5},{5,1},{9,13},{13,9},{2,6},{6,2},{1... | collective-permute-start | bytes 417800 | tf_op jit(solution)/shard_map/ppermute | solution.py:506
  24.2 13.4 %collective-permute-start.2 = (bf16[2,272,128]{2,1,0:T(8,128)(2,1)S(1)}, bf16[2,272,128]{2,1,0:T(8,128)(2,1)S(1)}, u32[]{:S(2)}, u32[]{:S(2)}) collective-permute-start(bf16[2,272,128]{2,1,0:T(8,128)(2,1)S(1)} %shard_map.69.refs_6_.mine_ref), channel_id=1, source_target_pairs={{0,8},{4,12},{8,0},{12,4},{1,9},{5,13},{9,1},{13,5},{2,10},{6,14},... | collective-permute-start | bytes 417800 | tf_op jit(solution)/shard_map/ppermute | solution.py:506
  24.7 5.2 %collective-permute-start.4 = (bf16[1,272,128]{2,1,0:T(8,128)(2,1)S(1)}, bf16[1,272,128]{2,1,0:T(8,128)(2,1)S(1)}, u32[]{:S(2)}, u32[]{:S(2)}) collective-permute-start(bf16[1,272,128]{2,1,0:T(8,128)(2,1)S(1)} %get-tuple-element.25._), channel_id=1, source_target_pairs={{0,4},{4,0},{8,12},{12,8},{1,5},{5,1},{9,13},{13,9},{2,6},{6,2},{1... | collective-permute-start | bytes 208904 | tf_op jit(solution)/shard_map/ppermute | solution.py:506
  28.1 5.6 %collective-permute-start.3 = (bf16[1,272,128]{2,1,0:T(8,128)(2,1)S(1)}, bf16[1,272,128]{2,1,0:T(8,128)(2,1)S(1)}, u32[]{:S(2)}, u32[]{:S(2)}) collective-permute-start(bf16[1,272,128]{2,1,0:T(8,128)(2,1)S(1)} %get-tuple-element.28._), channel_id=1, source_target_pairs={{0,4},{4,0},{8,12},{12,8},{1,5},{5,1},{9,13},{13,9},{2,6},{6,2},{1... | collective-permute-start | bytes 208904 | tf_op jit(solution)/shard_map/ppermute | solution.py:506
  30.2 8.1 %collective-permute-start.6 = (bf16[1,272,128]{2,1,0:T(8,128)(2,1)S(1)}, bf16[1,272,128]{2,1,0:T(8,128)(2,1)S(1)}, u32[]{:S(2)}, u32[]{:S(2)}) collective-permute-start(bf16[1,272,128]{2,1,0:T(8,128)(2,1)S(1)} %shard_map.71._.mine_ref), channel_id=1, source_target_pairs={{0,8},{4,12},{8,0},{12,4},{1,9},{5,13},{9,1},{13,5},{2,10},{6,14},... | collective-permute-start | bytes 208904 | tf_op jit(solution)/shard_map/ppermute | solution.py:506
  34.0 8.0 %collective-permute-start.8 = (bf16[1,272,128]{2,1,0:T(8,128)(2,1)S(1)}, bf16[1,272,128]{2,1,0:T(8,128)(2,1)S(1)}, u32[]{:S(2)}, u32[]{:S(2)}) collective-permute-start(bf16[1,272,128]{2,1,0:T(8,128)(2,1)S(1)} %shard_map.72._.mine_ref), channel_id=1, source_target_pairs={{0,8},{4,12},{8,0},{12,4},{1,9},{5,13},{9,1},{13,5},{2,10},{6,14},... | collective-permute-start | bytes 208904 | tf_op jit(solution)/shard_map/ppermute | solution.py:506
  38.2 8.5 %collective-permute-start.5 = (bf16[2,2,16,8,128]{4,3,2,1,0:T(8,128)(2,1)S(1)}, bf16[2,2,16,8,128]{4,3,2,1,0:T(8,128)(2,1)S(1)}, u32[]{:S(2)}, u32[]{:S(2)}) collective-permute-start(bf16[2,2,16,8,128]{4,3,2,1,0:T(8,128)(2,1)S(1)} %bitcast.7), channel_id=1, source_target_pairs={{0,4},{4,0},{8,12},{12,8},{1,5},{5,1},{9,13},{13,9},{2,6},{6,2},{1... | collective-permute-start | bytes 393224 | tf_op jit(solution)/shard_map/ppermute | solution.py:506
  38.6 6.2 %collective-permute-start.7 = (bf16[1,2,16,8,128]{4,3,2,1,0:T(8,128)(2,1)S(1)}, bf16[1,2,16,8,128]{4,3,2,1,0:T(8,128)(2,1)S(1)}, u32[]{:S(2)}, u32[]{:S(2)}) collective-permute-start(bf16[1,2,16,8,128]{4,3,2,1,0:T(8,128)(2,1)S(1)} %bitcast.9), channel_id=1, source_target_pairs={{0,4},{4,0},{8,12},{12,8},{1,5},{5,1},{9,13},{13,9},{2,6},{6,2},{1... | collective-permute-start | bytes 196616 | tf_op jit(solution)/shard_map/ppermute | solution.py:506
  42.3 4.3 %collective-permute-start.9 = (bf16[1,2,16,8,128]{4,3,2,1,0:T(8,128)(2,1)S(1)}, bf16[1,2,16,8,128]{4,3,2,1,0:T(8,128)(2,1)S(1)}, u32[]{:S(2)}, u32[]{:S(2)}) collective-permute-start(bf16[1,2,16,8,128]{4,3,2,1,0:T(8,128)(2,1)S(1)} %bitcast.11), channel_id=1, source_target_pairs={{0,4},{4,0},{8,12},{12,8},{1,5},{5,1},{9,13},{13,9},{2,6},{6,2},{1... | collective-permute-start | bytes 196616 | tf_op jit(solution)/shard_map/ppermute | solution.py:506

commit v3 on v2

--- a/solution.py
+++ b/solution.py
@@ -80,41 +80,62 @@
     return pltpu.with_memory_space_constraint(array, pltpu.HBM)
 
 
-def message_kernel(heads, suffix_ref, new_ref, out_ref, here, wide, sems):
+def message_kernel(
+    heads, owners, suffix_dev, tokens_dev,
+    suffix_ref, new_ref, prompt_ref, ancestors_ref, lengths_ref,
+    out_ref, bias_ref, keys_ref, here, wide, parents, extents, sems,
+):
     rows, each = suffix_ref.shape[1], new_ref.shape[2]
     total = here.shape[1]
-    count = (total - rows) // each
-    first = jnp.minimum(lax.axis_index("ctx") * count, new_ref.shape[0] - count)
-    copies = [pltpu.make_async_copy(suffix_ref, here.at[:, pl.ds(0, rows)], sems.at[0])]
-    for token in range(count):
-        there = here.at[:, pl.ds(rows + token * each, each)]
-        copies.append(pltpu.make_async_copy(new_ref.at[first + token], there, sems.at[1 + token]))
+    first = jnp.minimum(lax.axis_index("ctx") * tokens_dev, new_ref.shape[0] - tokens_dev)
+    small = [(ancestors_ref, parents), (lengths_ref, extents)]
+    parts = [(suffix_ref, here.at[:, pl.ds(0, rows)])]
+    for token in range(tokens_dev):
+        parts.append((new_ref.at[first + token], here.at[:, pl.ds(rows + token * each, each)]))
+    pairs = small + parts + [(prompt_ref.at[0], keys_ref)]
+    copies = [pltpu.make_async_copy(*pair, sems.at[i]) for i, pair in enumerate(pairs)]
     for copy in copies:
         copy.start()
-    for copy in copies:
+    for copy in copies[: len(small)]:
+        copy.wait()
+    bias_ref[...] = lineage_bias(
+        parents, extents, owners, parents.shape[1] // owners, suffix_dev, tokens_dev,
+        bias_ref.shape[1],
+    )
+    for copy in copies[len(small) : -1]:
         copy.wait()
     for kind in range(2):
         wide[kind] = here[kind].astype(jnp.float32)
         for head in range(heads):
             part = wide[kind, pl.ds(head, total // heads, stride=heads), :]
             out_ref[kind, head] = part.astype(out_ref.dtype)
-
-
-def build_message(suffix, new, heads, tokens_dev):
+    copies[-1].wait()
+
+
+def build_message(suffix, new, prompt, ancestors, lengths, heads, owners, suffix_dev, tokens_dev):
     rows = suffix.shape[1] + tokens_dev * new.shape[2]
     size = suffix.shape[2]
+    steps, particles = ancestors.shape
+    padded = round_up(particles * (suffix_dev + tokens_dev), LANES)
+    operands = (suffix, new, prompt, ancestors, lengths.reshape(1, -1))
     return pl.pallas_call(
-        functools.partial(message_kernel, heads),
-        in_specs=[pl.BlockSpec(memory_space=pltpu.HBM)] * 2,
-        out_shape=jax.ShapeDtypeStruct((2, heads, rows // heads, size), suffix.dtype),
+        functools.partial(message_kernel, heads, owners, suffix_dev, tokens_dev),
+        in_specs=[pl.BlockSpec(memory_space=pltpu.HBM)] * len(operands),
+        out_shape=(
+            jax.ShapeDtypeStruct((2, heads, rows // heads, size), suffix.dtype),
+            jax.ShapeDtypeStruct((steps * particles // owners, padded), jnp.float32),
+            jax.ShapeDtypeStruct(prompt.shape[1:], prompt.dtype),
+        ),
         scratch_shapes=[
             pltpu.VMEM((2, rows, size), suffix.dtype),
             pltpu.VMEM((2, rows, size), jnp.float32),
-            pltpu.SemaphoreType.DMA((1 + tokens_dev,)),
+            pltpu.VMEM(ancestors.shape, ancestors.dtype),
+            pltpu.VMEM((1, particles), lengths.dtype),
+            pltpu.SemaphoreType.DMA((4 + tokens_dev,)),
         ],
-        compiler_params=pltpu.CompilerParams(vmem_limit_bytes=16 << 20),
+        compiler_params=pltpu.CompilerParams(vmem_limit_bytes=24 << 20),
         cost_estimate=SMALL,
-    )(in_hbm(suffix), in_hbm(new))
+    )(*[in_hbm(operand) for operand in operands])
 
 
 def iota(shape, axis):
@@ -170,61 +191,48 @@
     return jnp.where(dot(mine, table, NN) > 0.5, 0.0, HIDDEN)
 
 
-def split_kernel(
-    heads, block, owners, suffix_dev, tokens_dev,
-    rows_ref, ancestors_ref, lengths_ref, out_ref, bias_ref, here, wide, sems,
-):
+def split_kernel(heads, block, rows_ref, keys_ref, out_ref, here, wide, sems):
     total = out_ref.shape[2]
-    places = [(kind, at) for kind in range(2) for at in range(0, total, block)]
+    places = range(0, total, block)
     copies = [
         pltpu.make_async_copy(
-            rows_ref.at[kind, pl.ds(at * heads, block * heads)],
-            here.at[kind, pl.ds(at * heads, block * heads)],
+            rows_ref.at[1, pl.ds(at * heads, block * heads)],
+            here.at[pl.ds(at * heads, block * heads)],
             sems.at[i],
         )
-        for i, (kind, at) in enumerate(places)
+        for i, at in enumerate(places)
     ]
     for copy in copies:
         copy.start()
-    bias_ref[...] = lineage_bias(
-        ancestors_ref,
-        lengths_ref,
-        owners,
-        ancestors_ref.shape[1] // owners,
-        suffix_dev,
-        tokens_dev,
-        bias_ref.shape[1],
-    )
-    for i, (kind, at) in enumerate(places):
-        copies[i].wait()
-        wide[i % 2] = here[kind, at * heads : (at + block) * heads].astype(jnp.float32)
-        for head in range(heads):
-            part = wide[i % 2, pl.ds(head, block, stride=heads), :]
-            out_ref[kind, head, at : at + block] = part.astype(out_ref.dtype)
-
-
-def split_prompt(rows, ancestors, lengths, heads, owners, suffix_dev, tokens_dev):
+    for kind, source in enumerate((keys_ref, here)):
+        for i, at in enumerate(places):
+            if kind == 1:
+                copies[i].wait()
+            wide[i % 2] = source[at * heads : (at + block) * heads].astype(jnp.float32)
+            for head in range(heads):
+                part = wide[i % 2, pl.ds(head, block, stride=heads), :]
+                out_ref[kind, head, at : at + block] = part.astype(out_ref.dtype)
+
+
+def split_prompt(rows, keys, heads):
     total = rows.shape[1] // heads
     block = math.gcd(total, 512)
     size = rows.shape[2]
-    steps, particles = ancestors.shape
-    padded = round_up(particles * (suffix_dev + tokens_dev), LANES)
     return pl.pallas_call(
-        functools.partial(split_kernel, heads, block, owners, suffix_dev, tokens_dev),
-        in_specs=[pl.BlockSpec(memory_space=pltpu.HBM)]
-        + [pl.BlockSpec(memory_space=pltpu.VMEM)] * 2,
-        out_shape=(
-            jax.ShapeDtypeStruct((2, heads, total, size), rows.dtype),
-            jax.ShapeDtypeStruct((steps * particles // owners, padded), jnp.float32),
-        ),
+        functools.partial(split_kernel, heads, block),
+        in_specs=[
+            pl.BlockSpec(memory_space=pltpu.HBM),
+            pl.BlockSpec(memory_space=pltpu.VMEM),
+        ],
+        out_shape=jax.ShapeDtypeStruct((2, heads, total, size), rows.dtype),
         scratch_shapes=[
-            pltpu.VMEM(rows.shape, rows.dtype),
+            pltpu.VMEM(rows.shape[1:], rows.dtype),
             pltpu.VMEM((2, block * heads, size), jnp.float32),
-            pltpu.SemaphoreType.DMA((2 * total // block,)),
+            pltpu.SemaphoreType.DMA((total // block,)),
         ],
         compiler_params=pltpu.CompilerParams(vmem_limit_bytes=24 << 20),
         cost_estimate=SMALL,
-    )(in_hbm(rows), ancestors, lengths.reshape(1, -1))
+    )(in_hbm(rows), keys)
 
 
 def with_ones(values):
@@ -242,15 +250,14 @@
 def prompt_sum(q, k_ref, v_ref, i, factor, peak):
     total = k_ref.shape[2]
     block = math.gcd(total, 512)
-    together = None
+    weights = []
     for at in range(0, total, block):
         scores = dot(q, k_ref[0, i, at : at + block], NT)
         if at == 0:
             top = row_peak(scores)
             offset = (top if peak is None else jnp.maximum(top, peak)) * factor
-        part = dot(weigh(scores, factor, offset), with_ones(v_ref[0, i, at : at + block]), NN)
-        together = part if together is None else together + part
-    return together, offset
+        weights.append(weigh(scores, factor, offset))
+    return dot(jnp.concatenate(weights, axis=1), with_ones(v_ref[0, i]), NN), offset
 
 
 def prompt_kernel(factor, q_ref, k_ref, v_ref, together_ref, offset_ref):
@@ -505,16 +512,23 @@
     def swap(value, bit):
         return lax.ppermute(value, "ctx", [(i, i ^ (1 << bit)) for i in range(shards)])
 
-    mine = build_message(
-        suffix_cache.reshape(2, -1, size), new_kv.reshape(steps, 2, -1, size), heads, tokens_dev
+    prompt_rows = prompt_cache.reshape(2, -1, size)
+    mine, bias, keys = build_message(
+        suffix_cache.reshape(2, -1, size),
+        new_kv.reshape(steps, 2, -1, size),
+        prompt_rows,
+        ancestors,
+        lengths,
+        heads,
+        owners,
+        suffix_dev,
+        tokens_dev,
     )
     row_list = [mine] + [
         lax.ppermute(mine, "dom", [(i, (i + hop) % owners) for i in range(owners)])
         for hop in range(1, owners)
     ]
-    prompt, bias = split_prompt(
-        prompt_cache.reshape(2, -1, size), ancestors, lengths, heads, owners, suffix_dev, tokens_dev
-    )
+    prompt = split_prompt(prompt_rows, keys, heads)
     last = [bias]
 
     def follow(results):

time: 47.2 us -> 47.9 us (1.015); the launches traced: 47.5 us -> 47 us
  local copies, waits for them, and re-layouts: 1.34 us -> 0.01 us
  starting transfers between devices: 16.3 us -> 17.3 us
    unnamed x6 -> x2, local copies, waits for them, and re-layouts: 1.34 us -> 0.01 us
    ppermute x9, starting transfers between devices: 13.3 us -> 14.3 us  [swap(): lax.ppermute(value, 'ctx', [(i, i ^ 1 << bit) for i in range(shards)])]
    ppermute x1, waiting for transfers between devices: 0.01 us -> 0.84 us  [on_device(): lax.ppermute(mine, 'dom', [(i, (i + hop) % owners) for i in range(owners)])]
    ppermute x9, waiting for transfers between devices: 6.87 us -> 6.14 us  [swap(): lax.ppermute(value, 'ctx', [(i, i ^ 1 << bit) for i in range(shards)])]
  transfers between devices with their start and end apart: 10 -> 10, of which waited for: 5 -> 5; matrix products, arithmetic and copies ran while one was open for 0% -> 0% of each run, Pallas kernels for 30% -> 35%
where the time goes in v3:
time: 47.9 us; the launch traced here: 47 us
  Pallas kernels  22.6 us (47%)
  starting transfers between devices  17.3 us (36%)
  waiting for transfers between devices  6.98 us (15%)
    ppermute x9, starting transfers between devices, swap(): lax.ppermute(value, 'ctx', [(i, i ^ 1 << bit) for i in range(shards)])  14.3 us
    pallas_call x3, Pallas kernels, attend(): pl.pallas_call(functools.partial(attend_kernel, factor, len(row_list), ha...  14.1 us
    ppermute x9, waiting for transfers between devices, swap(): lax.ppermute(value, 'ctx', [(i, i ^ 1 << bit) for i in range(shards)])  6.14 us
    ppermute x1, starting transfers between devices, on_device(): lax.ppermute(mine, 'dom', [(i, (i + hop) % owners) for i in range(owners)])  3 us
    pallas_call x1, Pallas kernels, build_message(): pl.pallas_call(functools.partial(message_kernel, heads, owners, suffix_de...  2.14 us
    pallas_call x1, Pallas kernels, split_prompt(): pl.pallas_call(functools.partial(split_kernel, heads, block), in_specs=[p...  1.74 us
    pallas_call x1, Pallas kernels, start_head(): pl.pallas_call(functools.partial(prompt_kernel, factor), grid=(1,), in_sp...  1.6 us
    pallas_call x3, Pallas kernels, merge_parts(): pl.pallas_call(functools.partial(merge_kernel, level, last), in_specs=in_...  1.13 us
  transfers between devices with their start and end apart: 10, of which 5 were waited for; matrix products, arithmetic and copies ran while one was open for 0% of the time, Pallas kernels for 35%

profile of v3, /device:TPU:0, one launch (start us, length us, event | category | flops | bytes accessed | tf_op | source)
XLA Modules:
  0.0 47.0 jit_solution(9420646065667644639)
XLA Ops:
  0.0 2.1 %shard_map.64 = (bf16[2,4,80,128]{3,2,1,0:T(8,128)(2,1)S(1)}, f32[64,256]{1,0:T(8,128)S(1)}, bf16[8192,128]{1,0:T(8,128)(2,1)S(1)}) custom-call(bf16[2,256,128]{2,1,0:T(8,128)(2,1)} %bitcast.15, bf16[4,2,64,128]{3,2,1,0:T(8,128)(2,1)} %bitcast.16, bf16[2,8192,128]{2,1,0:T(8,128)(2,1)} %bitcast.13, s32[4,32]{1,0:T(4,128)} %ancestors_ref.1, s32[1,32]{1,0:T(1,128)} %bitcast.17), custom_call_target="tpu_custom_call" | custom-call | bytes 4096 | tf_op jit(solution)/shard_map/pallas_call | solution.py:121
  2.1 3.0 %collective-permute-start = (bf16[2,4,80,128]{3,2,1,0:T(8,128)(2,1)S(1)}, bf16[2,4,80,128]{3,2,1,0:T(8,128)(2,1)S(1)}, u32[]{:S(2)}, u32[]{:S(2)}) collective-permute-start(bf16[2,4,80,128]{3,2,1,0:T(8,128)(2,1)S(1)} %get-tuple-element.21.refs_4_), channel_id=1, source_target_pairs={{0,2},{2,0},{1,3},{3,1},{4,6},{6,4},{5,7},{7,5},{8,10},{10,8},{9,1... | collective-permute-start | bytes 491528 | tf_op jit(solution)/shard_map/ppermute | solution.py:528
  5.2 0.0 copy-start
  5.2 1.7 %shard_map.65.k_ref.v_ref.refs_1_.refs_2_ = bf16[2,4,2048,128]{3,2,1,0:T(8,128)(2,1)S(1)} custom-call(bf16[2,8192,128]{2,1,0:T(8,128)(2,1)} %bitcast.14, bf16[8192,128]{1,0:T(8,128)(2,1)S(1)} %get-tuple-element.19.keys_ref), custom_call_target="tpu_custom_call" | custom-call | bytes 4096 | tf_op jit(solution)/shard_map/pallas_call | solution.py:221
  6.9 0.0 copy-done
  6.9 1.6 %shard_map.66 = (f32[512,256]{1,0:T(8,128)S(1)}, f32[512,128]{1,0:T(8,128)S(1)}) custom-call(bf16[4,16,4,8,128]{4,3,2,1,0:T(8,128)(2,1)S(1)} %copy-done, bf16[2,4,2048,128]{3,2,1,0:T(8,128)(2,1)S(1)} %shard_map.65.k_ref.v_ref.refs_1_.refs_2_, bf16[2,4,2048,128]{3,2,1,0:T(8,128)(2,1)S(1)} %shard_map.65.k_ref.v_ref.refs_1_.refs_2_), custom_call_target="tpu_custom_call" | custom-call | bytes 4096 | tf_op jit(solution)/shard_map/pallas_call | solution.py:293
  8.5 0.8 %collective-permute-done.refs_5_ = bf16[2,4,80,128]{3,2,1,0:T(8,128)(2,1)S(1)} collective-permute-done((bf16[2,4,80,128]{3,2,1,0:T(8,128)(2,1)S(1)}, bf16[2,4,80,128]{3,2,1,0:T(8,128)(2,1)S(1)}, u32[]{:S(2)}, u32[]{:S(2)}) %collective-permute-start) | collective-permute-done | bytes 163872 | tf_op jit(solution)/shard_map/ppermute | solution.py:528
  9.3 2.6 %shard_map.67 = (bf16[2,272,128]{2,1,0:T(8,128)(2,1)S(1)}, f32[2,256,128]{2,1,0:T(8,128)S(1)}, f32[2,256,128]{2,1,0:T(8,128)S(1)}) custom-call(bf16[4,16,4,8,128]{4,3,2,1,0:T(8,128)(2,1)S(1)} %copy-done, bf16[2,4,2048,128]{3,2,1,0:T(8,128)(2,1)S(1)} %shard_map.65.k_ref.v_ref.refs_1_.refs_2_, ...), custom_call_target="tpu_custom_call" | custom-call | bytes 4096 | tf_op jit(solution)/shard_map/pallas_call | solution.py:378
  12.0 5.6 %collective-permute-start.1 = (bf16[2,272,128]{2,1,0:T(8,128)(2,1)S(1)}, bf16[2,272,128]{2,1,0:T(8,128)(2,1)S(1)}, u32[]{:S(2)}, u32[]{:S(2)}) collective-permute-start(bf16[2,272,128]{2,1,0:T(8,128)(2,1)S(1)} %get-tuple-element.26.refs_6_), channel_id=1, source_target_pairs={{0,4},{4,0},{8,12},{12,8},{1,5},{5,1},{9,13},{13,9},{2,6},{6,2},{1... | collective-permute-start | bytes 417800 | tf_op jit(solution)/shard_map/ppermute | solution.py:513
  17.5 5.7 %shard_map.68 = (bf16[1,272,128]{2,1,0:T(8,128)(2,1)S(1)}, f32[1,256,128]{2,1,0:T(8,128)S(1)}, f32[1,256,128]{2,1,0:T(8,128)S(1)}) custom-call(bf16[4,16,4,8,128]{4,3,2,1,0:T(8,128)(2,1)S(1)} %copy-done, bf16[2,4,2048,128]{3,2,1,0:T(8,128)(2,1)S(1)} %shard_map.65.k_ref.v_ref.refs_1_.refs_2_, ...), custom_call_target="tpu_custom_call" | custom-call | bytes 4096 | tf_op jit(solution)/shard_map/pallas_call | solution.py:378
  23.2 0.0 collective-permute-done.1.got_ref
  23.3 0.5 %shard_map.69.refs_6_.mine_ref = bf16[2,272,128]{2,1,0:T(8,128)(2,1)S(1)} custom-call(f32[2,256,128]{2,1,0:T(8,128)S(1)} %get-tuple-element.24.keep_ref, f32[2,256,128]{2,1,0:T(8,128)S(1)} %get-tuple-element.25.sums_ref, bf16[2,272,128]{2,1,0:T(8,128)(2,1)S(1)} %collective-permute-done.1.got_ref, bf16[1,272,128]{2,1,0:T(8,128)(2,1)S(1)} %get-tuple-element.27._), custom_call_target="tpu_custom_call" | custom-call | bytes 4096 | tf_op jit(solution)/shard_map/pallas_call | solution.py:442
  23.7 0.1 collective-permute-start.2
  23.8 0.1 collective-permute-start.4
  23.9 5.7 %shard_map.70 = (bf16[1,272,128]{2,1,0:T(8,128)(2,1)S(1)}, f32[1,256,128]{2,1,0:T(8,128)S(1)}, f32[1,256,128]{2,1,0:T(8,128)S(1)}) custom-call(bf16[4,16,4,8,128]{4,3,2,1,0:T(8,128)(2,1)S(1)} %copy-done, bf16[2,4,2048,128]{3,2,1,0:T(8,128)(2,1)S(1)} %shard_map.65.k_ref.v_ref.refs_1_.refs_2_, ...), custom_call_target="tpu_custom_call" | custom-call | bytes 4096 | tf_op jit(solution)/shard_map/pallas_call | solution.py:378
  29.6 0.1 collective-permute-start.3
  29.7 0.0 collective-permute-done.4.got_ref
  29.7 0.3 shard_map.71._.mine_ref
  30.0 2.9 %collective-permute-start.6 = (bf16[1,272,128]{2,1,0:T(8,128)(2,1)S(1)}, bf16[1,272,128]{2,1,0:T(8,128)(2,1)S(1)}, u32[]{:S(2)}, u32[]{:S(2)}) collective-permute-start(bf16[1,272,128]{2,1,0:T(8,128)(2,1)S(1)} %shard_map.71._.mine_ref), channel_id=1, source_target_pairs={{0,8},{4,12},{8,0},{12,4},{1,9},{5,13},{9,1},{13,5},{2,10},{6,14},... | collective-permute-start | bytes 208904 | tf_op jit(solution)/shard_map/ppermute | solution.py:513
  32.9 1.1 %collective-permute-done.3.got_ref = bf16[1,272,128]{2,1,0:T(8,128)(2,1)S(1)} collective-permute-done((bf16[1,272,128]{2,1,0:T(8,128)(2,1)S(1)}, bf16[1,272,128]{2,1,0:T(8,128)(2,1)S(1)}, u32[]{:S(2)}, u32[]{:S(2)}) %collective-permute-start.3) | collective-permute-done | bytes 69664 | tf_op jit(solution)/shard_map/ppermute | solution.py:513
  34.0 0.3 shard_map.72._.mine_ref
  34.3 3.5 %collective-permute-start.8 = (bf16[1,272,128]{2,1,0:T(8,128)(2,1)S(1)}, bf16[1,272,128]{2,1,0:T(8,128)(2,1)S(1)}, u32[]{:S(2)}, u32[]{:S(2)}) collective-permute-start(bf16[1,272,128]{2,1,0:T(8,128)(2,1)S(1)} %shard_map.72._.mine_ref), channel_id=1, source_target_pairs={{0,8},{4,12},{8,0},{12,4},{1,9},{5,13},{9,1},{13,5},{2,10},{6,14},... | collective-permute-start | bytes 208904 | tf_op jit(solution)/shard_map/ppermute | solution.py:513
  37.8 0.0 collective-permute-done.2.got_ref
  37.8 0.5 shard_map.73._
  38.3 0.1 collective-permute-start.5
  38.3 0.0 collective-permute-done.6.got_ref
  38.4 0.3 shard_map.74._
  38.7 2.1 %collective-permute-done.8.got_ref = bf16[1,272,128]{2,1,0:T(8,128)(2,1)S(1)} collective-permute-done((bf16[1,272,128]{2,1,0:T(8,128)(2,1)S(1)}, bf16[1,272,128]{2,1,0:T(8,128)(2,1)S(1)}, u32[]{:S(2)}, u32[]{:S(2)}) %collective-permute-start.8) | collective-permute-done | bytes 69664 | tf_op jit(solution)/shard_map/ppermute | solution.py:513
  40.8 0.3 shard_map.75
  41.2 0.4 collective-permute-start.9
  41.6 1.7 %collective-permute-start.7 = (bf16[1,2,16,8,128]{4,3,2,1,0:T(8,128)(2,1)S(1)}, bf16[1,2,16,8,128]{4,3,2,1,0:T(8,128)(2,1)S(1)}, u32[]{:S(2)}, u32[]{:S(2)}) collective-permute-start(bf16[1,2,16,8,128]{4,3,2,1,0:T(8,128)(2,1)S(1)} %bitcast.9), channel_id=1, source_target_pairs={{0,4},{4,0},{8,12},{12,8},{1,5},{5,1},{9,13},{13,9},{2,6},{6,2},{1... | collective-permute-start | bytes 196616 | tf_op jit(solution)/shard_map/ppermute | solution.py:513
  43.3 2.2 %collective-permute-done.9.refs_5_ = bf16[1,2,16,8,128]{4,3,2,1,0:T(8,128)(2,1)S(1)} collective-permute-done((bf16[1,2,16,8,128]{4,3,2,1,0:T(8,128)(2,1)S(1)}, bf16[1,2,16,8,128]{4,3,2,1,0:T(8,128)(2,1)S(1)}, u32[]{:S(2)}, u32[]{:S(2)}) %collective-permute-start.9) | collective-permute-done | bytes 65568 | tf_op jit(solution)/shard_map/ppermute | solution.py:513
  45.5 0.7 %collective-permute-done.7.refs_3_ = bf16[1,2,16,8,128]{4,3,2,1,0:T(8,128)(2,1)S(1)} collective-permute-done((bf16[1,2,16,8,128]{4,3,2,1,0:T(8,128)(2,1)S(1)}, bf16[1,2,16,8,128]{4,3,2,1,0:T(8,128)(2,1)S(1)}, u32[]{:S(2)}, u32[]{:S(2)}) %collective-permute-start.7) | collective-permute-done | bytes 65568 | tf_op jit(solution)/shard_map/ppermute | solution.py:513
  46.2 0.0 collective-permute-done.5.refs_1_
  46.2 0.8 %shard_map.76 = bf16[4,16,4,8,128]{4,3,2,1,0:T(8,128)(2,1)} custom-call(bf16[2,2,16,8,128]{4,3,2,1,0:T(8,128)(2,1)S(1)} %bitcast.8, bf16[2,2,16,8,128]{4,3,2,1,0:T(8,128)(2,1)S(1)} %collective-permute-done.5.refs_1_, bf16[1,2,16,8,128]{4,3,2,1,0:T(8,128)(2,1)S(1)} %bitcast.10, bf16[1,2,16,8,128]{4,3,2,1,0:T(8,128)(2,1)S(1)} %collective-permute-done.7.refs_3_, ...), custom_call_target="tpu_custom_call" | custom-call | bytes 4096 | tf_op jit(solution)/shard_map/pallas_call | solution.py:492
Async XLA Ops:
  2.1 7.2 %collective-permute-start = (bf16[2,4,80,128]{3,2,1,0:T(8,128)(2,1)S(1)}, bf16[2,4,80,128]{3,2,1,0:T(8,128)(2,1)S(1)}, u32[]{:S(2)}, u32[]{:S(2)}) collective-permute-start(bf16[2,4,80,128]{3,2,1,0:T(8,128)(2,1)S(1)} %get-tuple-element.21.refs_4_), channel_id=1, source_target_pairs={{0,2},{2,0},{1,3},{3,1},{4,6},{6,4},{5,7},{7,5},{8,10},{10,8},{9,1... | collective-permute-start | bytes 491528 | tf_op jit(solution)/shard_map/ppermute | solution.py:528
  5.2 1.8 %copy-start = (bf16[4,16,4,8,128]{4,3,2,1,0:T(8,128)(2,1)S(1)}, bf16[4,16,4,8,128]{4,3,2,1,0:T(8,128)(2,1)}, u32[]{:S(2)}) copy-start(bf16[4,16,4,8,128]{4,3,2,1,0:T(8,128)(2,1)} %refs_0_.5) | copy-start | bytes 1572868
  12.0 11.3 %collective-permute-start.1 = (bf16[2,272,128]{2,1,0:T(8,128)(2,1)S(1)}, bf16[2,272,128]{2,1,0:T(8,128)(2,1)S(1)}, u32[]{:S(2)}, u32[]{:S(2)}) collective-permute-start(bf16[2,272,128]{2,1,0:T(8,128)(2,1)S(1)} %get-tuple-element.26.refs_6_), channel_id=1, source_target_pairs={{0,4},{4,0},{8,12},{12,8},{1,5},{5,1},{9,13},{13,9},{2,6},{6,2},{1... | collective-permute-start | bytes 417800 | tf_op jit(solution)/shard_map/ppermute | solution.py:513
  23.7 14.1 %collective-permute-start.2 = (bf16[2,272,128]{2,1,0:T(8,128)(2,1)S(1)}, bf16[2,272,128]{2,1,0:T(8,128)(2,1)S(1)}, u32[]{:S(2)}, u32[]{:S(2)}) collective-permute-start(bf16[2,272,128]{2,1,0:T(8,128)(2,1)S(1)} %shard_map.69.refs_6_.mine_ref), channel_id=1, source_target_pairs={{0,8},{4,12},{8,0},{12,4},{1,9},{5,13},{9,1},{13,5},{2,10},{6,14},... | collective-permute-start | bytes 417800 | tf_op jit(solution)/shard_map/ppermute | solution.py:513
  23.8 5.9 %collective-permute-start.4 = (bf16[1,272,128]{2,1,0:T(8,128)(2,1)S(1)}, bf16[1,272,128]{2,1,0:T(8,128)(2,1)S(1)}, u32[]{:S(2)}, u32[]{:S(2)}) collective-permute-start(bf16[1,272,128]{2,1,0:T(8,128)(2,1)S(1)} %get-tuple-element.27._), channel_id=1, source_target_pairs={{0,4},{4,0},{8,12},{12,8},{1,5},{5,1},{9,13},{13,9},{2,6},{6,2},{1... | collective-permute-start | bytes 208904 | tf_op jit(solution)/shard_map/ppermute | solution.py:513
  29.6 4.4 %collective-permute-start.3 = (bf16[1,272,128]{2,1,0:T(8,128)(2,1)S(1)}, bf16[1,272,128]{2,1,0:T(8,128)(2,1)S(1)}, u32[]{:S(2)}, u32[]{:S(2)}) collective-permute-start(bf16[1,272,128]{2,1,0:T(8,128)(2,1)S(1)} %get-tuple-element.30._), channel_id=1, source_target_pairs={{0,4},{4,0},{8,12},{12,8},{1,5},{5,1},{9,13},{13,9},{2,6},{6,2},{1... | collective-permute-start | bytes 208904 | tf_op jit(solution)/shard_map/ppermute | solution.py:513
  30.0 8.3 %collective-permute-start.6 = (bf16[1,272,128]{2,1,0:T(8,128)(2,1)S(1)}, bf16[1,272,128]{2,1,0:T(8,128)(2,1)S(1)}, u32[]{:S(2)}, u32[]{:S(2)}) collective-permute-start(bf16[1,272,128]{2,1,0:T(8,128)(2,1)S(1)} %shard_map.71._.mine_ref), channel_id=1, source_target_pairs={{0,8},{4,12},{8,0},{12,4},{1,9},{5,13},{9,1},{13,5},{2,10},{6,14},... | collective-permute-start | bytes 208904 | tf_op jit(solution)/shard_map/ppermute | solution.py:513
  34.3 6.5 %collective-permute-start.8 = (bf16[1,272,128]{2,1,0:T(8,128)(2,1)S(1)}, bf16[1,272,128]{2,1,0:T(8,128)(2,1)S(1)}, u32[]{:S(2)}, u32[]{:S(2)}) collective-permute-start(bf16[1,272,128]{2,1,0:T(8,128)(2,1)S(1)} %shard_map.72._.mine_ref), channel_id=1, source_target_pairs={{0,8},{4,12},{8,0},{12,4},{1,9},{5,13},{9,1},{13,5},{2,10},{6,14},... | collective-permute-start | bytes 208904 | tf_op jit(solution)/shard_map/ppermute | solution.py:513
  38.3 7.9 %collective-permute-start.5 = (bf16[2,2,16,8,128]{4,3,2,1,0:T(8,128)(2,1)S(1)}, bf16[2,2,16,8,128]{4,3,2,1,0:T(8,128)(2,1)S(1)}, u32[]{:S(2)}, u32[]{:S(2)}) collective-permute-start(bf16[2,2,16,8,128]{4,3,2,1,0:T(8,128)(2,1)S(1)} %bitcast.7), channel_id=1, source_target_pairs={{0,4},{4,0},{8,12},{12,8},{1,5},{5,1},{9,13},{13,9},{2,6},{6,2},{1... | collective-permute-start | bytes 393224 | tf_op jit(solution)/shard_map/ppermute | solution.py:513
  41.2 4.3 %collective-permute-start.9 = (bf16[1,2,16,8,128]{4,3,2,1,0:T(8,128)(2,1)S(1)}, bf16[1,2,16,8,128]{4,3,2,1,0:T(8,128)(2,1)S(1)}, u32[]{:S(2)}, u32[]{:S(2)}) collective-permute-start(bf16[1,2,16,8,128]{4,3,2,1,0:T(8,128)(2,1)S(1)} %bitcast.11), channel_id=1, source_target_pairs={{0,4},{4,0},{8,12},{12,8},{1,5},{5,1},{9,13},{13,9},{2,6},{6,2},{1... | collective-permute-start | bytes 196616 | tf_op jit(solution)/shard_map/ppermute | solution.py:513
  41.6 4.6 %collective-permute-start.7 = (bf16[1,2,16,8,128]{4,3,2,1,0:T(8,128)(2,1)S(1)}, bf16[1,2,16,8,128]{4,3,2,1,0:T(8,128)(2,1)S(1)}, u32[]{:S(2)}, u32[]{:S(2)}) collective-permute-start(bf16[1,2,16,8,128]{4,3,2,1,0:T(8,128)(2,1)S(1)} %bitcast.9), channel_id=1, source_target_pairs={{0,4},{4,0},{8,12},{12,8},{1,5},{5,1},{9,13},{13,9},{2,6},{6,2},{1... | collective-permute-start | bytes 196616 | tf_op jit(solution)/shard_map/ppermute | solution.py:513
